TPU v7x, 128 devices: a whole 4x4x4 slice. The times are simulated.
128 devices in a mesh: gauss: 16 (over y_hi, z, core), img: 8 (over y_lo, x).
Axes of the slice: x: 4, y: 4 (y_hi: 2, y_lo: 2; y = y_hi * 2 + y_lo), z: 4, core: 2. Of those that a mesh axis runs over, the one named last changes fastest.
Arguments:
- observed: bfloat16 [32, 256, 256], P('img', 'gauss'), may hold values from -6 to 6
- pose_index: int32 [32], P('img'), may hold values from 0 to 4095
- batch_order: int32 [32], P('img'), may hold values from 0 to 3, as said below
- latents: float32 [32, 16], P('img'), may hold values from -3 to 3
- base_positions: float32 [3, 131072], P(None, 'gauss'), may hold values from -70 to 69
- amplitudes: float32 [131072], P('gauss'), may hold values from -0.875 to 0.875
- widths: float32 [131072], P('gauss'), may hold values from 1 to 3
- deform_modes: float32 [16, 3, 131072], P(None, None, ('gauss', 'img')), may hold values from -12 to 12
Outputs:
- final_residual: float32 [8, 256, 256], P('img', 'gauss')
- new_modes: float32 [16, 3, 131072], P(None, None, ('gauss', 'img'))
Inputs may be any that keep to these rules, and one draw needn't show every extreme that they name: `batch_order`: in each aligned block of 4 entries (one device's images) every number from 0 to 3 appears exactly once.
All inputs are finite; a program needn't handle non-finite values.
Results may differ from a plain program's by a relative error of at most 0.0045.
Values may be sent and summed in bfloat16 or wider, within the bound.
A program may use at most 64 MiB of HBM per device.

v0:
```python
import math

import jax
import jax.numpy as jnp
from jax import lax
from jax.sharding import PartitionSpec as P

PIX = 256
K = 16
NROT = 4096
STEPS = 2


step_size = 0.5
tiny_eps = 1e-06


def copy_for_each(value, axis):
    devices = lax.axis_size(axis)
    return lax.all_to_all(
        jnp.broadcast_to(value[None], (devices, *value.shape)), axis, 0, 0, tiled=True
    )


def joined_along(parts, dim):
    parts = jnp.moveaxis(parts, 0, dim)
    shape = parts.shape
    return parts.reshape(*shape[:dim], shape[dim] * shape[dim + 1], *shape[dim + 2 :])


def collect(value, axis, dim):
    parts = copy_for_each(value, axis)
    return joined_along(parts, dim)


def split_up(value, dim, devices):
    shape = value.shape
    parts = value.reshape(*shape[:dim], devices, shape[dim] // devices, *shape[dim + 1 :])
    return jnp.moveaxis(parts, dim, 0)


def sum_at_owner(value, axis, dim):
    devices = lax.axis_size(axis)
    parts = lax.all_to_all(split_up(value, dim, devices), axis, 0, 0, tiled=True)
    return jnp.sum(parts, axis=0)


def sent_together(arrays, axis, dim, along):
    columns = [a.reshape(*a.shape[:along], -1) for a in arrays]
    both = jnp.concatenate(columns, axis=along)
    filled, at, finished = (collect(both, axis, dim), 0, [])
    for a, column in zip(arrays, columns):
        share = filled[..., at : at + column.shape[along]]
        finished.append(share.reshape(*share.shape[:along], *a.shape[along:]))
        at += column.shape[along]
    return tuple(finished)


def taken_together(value, axis):
    return copy_for_each(value, axis).sum(axis=0)


def rotation_rows(pose_id):
    cos_beta = 1.0 - (2 * pose_id + 1).astype(jnp.float32) / NROT
    sin_beta = jnp.sqrt(1.0 - cos_beta * cos_beta)
    alpha = (pose_id * 55 % 144).astype(jnp.float32) * (2.0 * math.pi / 144.0)
    gamma = (pose_id % 8).astype(jnp.float32) * (math.pi / 4.0)
    cos_alpha, sin_alpha = (jnp.cos(alpha), jnp.sin(alpha))
    cos_gamma, sin_gamma = (jnp.cos(gamma), jnp.sin(gamma))
    first = jnp.stack(
        [
            cos_alpha * cos_beta * cos_gamma - sin_alpha * sin_gamma,
            -cos_alpha * cos_beta * sin_gamma - sin_alpha * cos_gamma,
            cos_alpha * sin_beta,
        ]
    )
    second = jnp.stack(
        [
            sin_alpha * cos_beta * cos_gamma + cos_alpha * sin_gamma,
            -sin_alpha * cos_beta * sin_gamma + cos_alpha * cos_gamma,
            sin_alpha * sin_beta,
        ]
    )
    return jnp.stack([first, second])


def factors(positions, rotation, amplitudes, widths):
    center = (PIX - 1) * 0.5
    proj_u = (
        rotation[0, 0] * positions[0]
        + rotation[0, 1] * positions[1]
        + rotation[0, 2] * positions[2]
        + center
    )
    proj_v = (
        rotation[1, 0] * positions[0]
        + rotation[1, 1] * positions[1]
        + rotation[1, 2] * positions[2]
        + center
    )
    pixels = jnp.arange(PIX).astype(jnp.float32)
    inv_var = 1.0 / (widths * widths)
    diff_u = pixels[None, :] - proj_u[:, None]
    diff_v = pixels[None, :] - proj_v[:, None]
    profile_u = jnp.exp(-0.5 * diff_u * diff_u * inv_var[:, None]).astype(jnp.bfloat16)
    profile_v = (amplitudes[:, None] * jnp.exp(-0.5 * diff_v * diff_v * inv_var[:, None])).astype(
        jnp.bfloat16
    )
    return (profile_u, profile_v, diff_u, diff_v, inv_var)


def body(
    observed, pose_index, batch_order, latents, base_positions, amplitudes, widths, deform_modes
):
    own_share = deform_modes.shape[2]
    entries = 3 * K * base_positions.shape[1] * lax.axis_size("gauss")
    full_modes = collect(deform_modes, "img", 2)
    final_rows = None
    for outer in range(STEPS):
        chosen = batch_order[outer]
        rotation = rotation_rows(pose_index[chosen])
        latent = latents[chosen]
        positions = base_positions + jnp.einsum(
            "k,kcg->cg", latent, full_modes, precision=lax.Precision.HIGHEST
        )
        profile_u, profile_v, diff_u, diff_v, inv_var = factors(
            positions, rotation, amplitudes, widths
        )
        measured = observed[chosen]
        image_rows = sum_at_owner(
            lax.dot_general(
                profile_u, profile_v, (((0,), (0,)), ((), ())), preferred_element_type=jnp.float32
            ),
            "gauss",
            0,
        )
        residual = image_rows - measured.astype(jnp.float32)
        final_rows = residual
        whole_b = collect(residual.astype(jnp.bfloat16), "gauss", 0)
        weighted_u = lax.dot_general(
            profile_v, whole_b, (((1,), (1,)), ((), ())), preferred_element_type=jnp.float32
        )
        weighted_v = jnp.dot(profile_u, whole_b, preferred_element_type=jnp.float32)
        grad_u = inv_var * jnp.sum(profile_u.astype(jnp.float32) * diff_u * weighted_u, axis=1)
        grad_v = inv_var * jnp.sum(profile_v.astype(jnp.float32) * diff_v * weighted_v, axis=1)
        shift_grad = jnp.stack(
            [rotation[0, c] * grad_u + rotation[1, c] * grad_v for c in range(3)]
        )
        pieces = sent_together((shift_grad[None], latent[None]), "img", 0, 1)
        mode_grad = jnp.einsum("ik,icg->kcg", pieces[1], pieces[0], precision=lax.Precision.HIGHEST)
        squares = taken_together(jnp.sum(mode_grad * mode_grad), "gauss")
        full_modes = full_modes - step_size * mode_grad / jnp.sqrt(squares / entries + tiny_eps)
    out_modes = lax.dynamic_slice_in_dim(
        full_modes, lax.axis_index("img") * own_share, own_share, 2
    )
    return (final_rows[None], out_modes)


def solution(mesh):
    return jax.shard_map(
        body,
        mesh=mesh,
        in_specs=(
            P("img", "gauss", None),
            P("img"),
            P("img"),
            P("img", None),
            P(None, "gauss"),
            P("gauss"),
            P("gauss"),
            P(None, None, ("gauss", "img")),
        ),
        out_specs=(P("img", "gauss", None), P(None, None, ("gauss", "img"))),
        check_vma=False,
    )
```

profile of v0, /device:TPU:1, one launch (start us, length us, event | category | flops | bytes accessed | tf_op | source)
XLA Modules:
  0.0 199.6 jit_solution(13688851207578977981)
XLA Ops:
  2.9 6.0 %all-to-all-start = ((f32[8,16,3,1024]{3,1,2,0:T(8,128)}), f32[8,16,3,1024]{3,1,2,0:T(8,128)S(1)}, u32[]{:S(2)}, u32[]{:S(2)}) async-start(f32[8,16,3,1024]{3,1,2,0:T(8,128)} %broadcast_in_dim.22), calls=%async_computation | async-start | bytes 3145728 | tf_op jit(solution)/shard_map/all_to_all | solution.py:20
  19.1 11.2 %all-to-all-done = f32[8,16,3,1024]{3,1,2,0:T(8,128)S(1)} async-done(((f32[8,16,3,1024]{3,1,2,0:T(8,128)}), f32[8,16,3,1024]{3,1,2,0:T(8,128)S(1)}, u32[]{:S(2)}, u32[]{:S(2)}) %all-to-all-start) | async-done | bytes 1572896 | tf_op jit(solution)/shard_map/all_to_all | solution.py:20
  31.5 3.8 %add_add_fusion.2 = (f32[1,8192]{1,0:T(1,128)S(1)}, f32[1,8192]{1,0:T(1,128)S(1)}) fusion(f32[3,8192]{1,0:T(4,128)S(1)} %bitcast_add_fusion.1, f32[]{:T(128)} %bitcast.29, f32[]{:T(128)} %bitcast.28, f32[]{:T(128)} %bitcast.27, f32[]{:T(128)} %bitcast.21, f32[]{:T(128)} %bitcast.20, f32[]{:T(128)} %bitcast.16), kind=kLoop, calls=%fused_computation.58 | loop fusion | flops 98304 | bytes 163864 | tf_op jit(solution)/shard_map/add | solution.py:96
  35.4 4.0 %fusion.18 = f32[256,256]{1,0:T(8,128)S(1)} fusion(f32[8192]{0:T(1024)S(1)} %multiply_divide_fusion, f32[8192]{0:T(1024)S(1)} %bitcast.146, f32[256]{0:T(256)S(1)} %iota_convert_fusion, f32[8192]{0:T(1024)S(1)} %bitcast.143, f32[8192]{0:T(1024)S(1)} %copy-done.6), kind=kOutput, calls=%fused_computation.31 | convolution fusion | flops 1096810496 | bytes 394240 | tf_op jit(solution)/shard_map/dot_general | solution.py:131
  39.4 17.0 %all_to_all.47 = f32[16,16,256]{2,1,0:T(8,128)S(1)} all-to-all(f32[16,16,256]{2,1,0:T(8,128)S(1)} %bitcast.125), channel_id=1, replica_groups=mesh['gauss'=16,'img'=8] {'gauss'}, dimensions={0} | all-to-all | bytes 524288 | tf_op jit(solution)/shard_map/all_to_all | solution.py:44
  56.4 11.1 %all_to_all.48 = bf16[16,16,256]{2,1,0:T(8,128)(2,1)S(1)} all-to-all(bf16[16,16,256]{2,1,0:T(8,128)(2,1)S(1)} %broadcast_in_dim.24), channel_id=1, replica_groups=mesh['gauss'=16,'img'=8] {'gauss'}, dimensions={0} | all-to-all | bytes 262144 | tf_op jit(solution)/shard_map/all_to_all | solution.py:20
  67.5 5.1 %fusion.30 = f32[8192]{0:T(1024)S(1)} fusion(bf16[256,256]{1,0:T(8,128)(2,1)S(1)} %bitcast.135, f32[8192]{0:T(1024)S(1)} %bitcast.144, f32[8192]{0:T(1024)S(1)} %copy-done.6, f32[8192]{0:T(1024)S(1)} %multiply_divide_fusion, f32[256]{0:T(256)S(1)} %iota_convert_fusion, f32[8192]{0:T(1024)S(1)} %bitcast.147), kind=kOutput, calls=%fused_computation.34 | convolution fusion | flops 1105190912 | bytes 295936 | tf_op jit(solution)/shard_map/dot_general | solution.py:140
  72.6 5.0 %fusion.24 = f32[8192]{0:T(1024)S(1)} fusion(bf16[256,256]{1,0:T(8,128)(2,1)S(1)} %bitcast.136, f32[8192]{0:T(1024)S(1)} %multiply_divide_fusion, f32[8192]{0:T(1024)S(1)} %bitcast.148, f32[256]{0:T(256)S(1)} %iota_convert_fusion, f32[8192]{0:T(1024)S(1)} %bitcast.145, f32[8192]{0:T(1024)S(1)} %copy-done.6), kind=kOutput, calls=%fused_computation.32 | convolution fusion | flops 1105190912 | bytes 295936 | tf_op jit(solution)/shard_map/dot_general | solution.py:143
  77.7 3.7 %multiply_add_fusion.5 = (f32[8192]{0:T(1024)S(1)}, f32[8192]{0:T(1024)S(1)}, f32[8192]{0:T(1024)S(1)}) fusion(f32[]{:T(128)} %bitcast.27, f32[]{:T(128)} %bitcast.16, f32[8192]{0:T(1024)S(1)} %fusion.24, f32[8192]{0:T(1024)S(1)} %fusion.30, f32[8192]{0:T(1024)S(1)} %copy-done.1, f32[]{:T(128)} %bitcast.28, f32[]{:T(128)} %bitcast.20, f32[]{:T(128)} %bitcast.29, ...), kind=kLoop, calls=%fused_computation.57 | loop fusion | flops 106496 | bytes 196632 | tf_op jit(solution)/shard_map/add | solution.py:147
  83.2 3.5 %all-to-all-start.3 = ((f32[8,1,24592]{2,1,0:T(1,128)}), f32[8,1,24592]{2,1,0:T(1,128)S(1)}, u32[]{:S(2)}, u32[]{:S(2)}) async-start(f32[8,1,24592]{2,1,0:T(1,128)} %broadcast_in_dim.26), calls=%async_computation.3 | async-start | bytes 1581056 | tf_op jit(solution)/shard_map/all_to_all | solution.py:20
  91.1 8.6 %all-to-all-done.3 = f32[8,1,24592]{2,1,0:T(1,128)S(1)} async-done(((f32[8,1,24592]{2,1,0:T(1,128)}), f32[8,1,24592]{2,1,0:T(1,128)S(1)}, u32[]{:S(2)}, u32[]{:S(2)}) %all-to-all-start.3) | async-done | bytes 786976 | tf_op jit(solution)/shard_map/all_to_all | solution.py:20
  104.3 4.1 %all-to-all-start.4 = ((f32[16,1,1]{2,1,0:T(1,128)}), f32[16,1,1]{2,1,0:T(1,128)S(1)}, u32[]{:S(2)}, u32[]{:S(2)}) async-start(f32[16,1,1]{2,1,0:T(1,128)} %broadcast_in_dim.27), calls=%async_computation.4 | async-start | bytes 16384 | tf_op jit(solution)/shard_map/all_to_all | solution.py:20
  109.0 6.3 %all-to-all-done.4 = f32[16,1,1]{2,1,0:T(1,128)S(1)} async-done(((f32[16,1,1]{2,1,0:T(1,128)}), f32[16,1,1]{2,1,0:T(1,128)S(1)}, u32[]{:S(2)}, u32[]{:S(2)}) %all-to-all-start.4) | async-done | bytes 96 | tf_op jit(solution)/shard_map/all_to_all | solution.py:20
  119.2 3.8 %add_add_fusion = (f32[1,8192]{1,0:T(1,128)S(1)}, f32[1,8192]{1,0:T(1,128)S(1)}) fusion(f32[3,8192]{1,0:T(4,128)S(1)} %bitcast_add_fusion, f32[]{:T(128)} %bitcast.50, f32[]{:T(128)} %bitcast.49, f32[]{:T(128)} %bitcast.48, f32[]{:T(128)} %bitcast.42, f32[]{:T(128)} %bitcast.41, f32[]{:T(128)} %bitcast.6), kind=kLoop, calls=%fused_computation.53 | loop fusion | flops 98304 | bytes 163864 | tf_op jit(solution)/shard_map/add | solution.py:96
  123.0 4.0 %fusion.15 = f32[256,256]{1,0:T(8,128)S(1)} fusion(f32[8192]{0:T(1024)S(1)} %bitcast.140, f32[8192]{0:T(1024)S(1)} %multiply_divide_fusion, f32[256]{0:T(256)S(1)} %iota_convert_fusion, f32[8192]{0:T(1024)S(1)} %bitcast.137, f32[8192]{0:T(1024)S(1)} %copy-done.6), kind=kOutput, calls=%fused_computation.30 | convolution fusion | flops 1096810496 | bytes 394240 | tf_op jit(solution)/shard_map/dot_general | solution.py:131
  127.0 11.8 %all_to_all.49 = f32[16,16,256]{2,1,0:T(8,128)S(1)} all-to-all(f32[16,16,256]{2,1,0:T(8,128)S(1)} %bitcast.126), channel_id=1, replica_groups=mesh['gauss'=16,'img'=8] {'gauss'}, dimensions={0} | all-to-all | bytes 524288 | tf_op jit(solution)/shard_map/all_to_all | solution.py:44
  139.5 11.1 %all_to_all.50 = bf16[16,16,256]{2,1,0:T(8,128)(2,1)S(1)} all-to-all(bf16[16,16,256]{2,1,0:T(8,128)(2,1)S(1)} %broadcast_in_dim.29), channel_id=1, replica_groups=mesh['gauss'=16,'img'=8] {'gauss'}, dimensions={0} | all-to-all | bytes 262144 | tf_op jit(solution)/shard_map/all_to_all | solution.py:20
  150.6 5.1 %fusion.33 = f32[8192]{0:T(1024)S(1)} fusion(bf16[256,256]{1,0:T(8,128)(2,1)S(1)} %bitcast.133, f32[8192]{0:T(1024)S(1)} %bitcast.138, f32[8192]{0:T(1024)S(1)} %copy-done.6, f32[8192]{0:T(1024)S(1)} %multiply_divide_fusion, f32[256]{0:T(256)S(1)} %iota_convert_fusion, f32[8192]{0:T(1024)S(1)} %bitcast.141), kind=kOutput, calls=%fused_computation.35 | convolution fusion | flops 1105190912 | bytes 295936 | tf_op jit(solution)/shard_map/dot_general | solution.py:140
  155.7 5.0 %fusion.27 = f32[8192]{0:T(1024)S(1)} fusion(bf16[256,256]{1,0:T(8,128)(2,1)S(1)} %bitcast.134, f32[8192]{0:T(1024)S(1)} %bitcast.142, f32[8192]{0:T(1024)S(1)} %multiply_divide_fusion, f32[256]{0:T(256)S(1)} %iota_convert_fusion, f32[8192]{0:T(1024)S(1)} %bitcast.139, f32[8192]{0:T(1024)S(1)} %copy-done.6), kind=kOutput, calls=%fused_computation.33 | convolution fusion | flops 1105190912 | bytes 295936 | tf_op jit(solution)/shard_map/dot_general | solution.py:143
  160.7 3.7 %multiply_add_fusion.2 = (f32[8192]{0:T(1024)S(1)}, f32[8192]{0:T(1024)S(1)}, f32[8192]{0:T(1024)S(1)}) fusion(f32[]{:T(128)} %bitcast.48, f32[]{:T(128)} %bitcast.6, f32[8192]{0:T(1024)S(1)} %fusion.27, f32[8192]{0:T(1024)S(1)} %fusion.33, f32[8192]{0:T(1024)S(1)} %copy-done.1, f32[]{:T(128)} %bitcast.49, f32[]{:T(128)} %bitcast.41, f32[]{:T(128)} %bitcast.50, ...), kind=kLoop, calls=%fused_computation.52 | loop fusion | flops 106496 | bytes 196632 | tf_op jit(solution)/shard_map/add | solution.py:147
  166.2 3.5 %all-to-all-start.7 = ((f32[8,1,24592]{2,1,0:T(1,128)}), f32[8,1,24592]{2,1,0:T(1,128)S(1)}, u32[]{:S(2)}, u32[]{:S(2)}) async-start(f32[8,1,24592]{2,1,0:T(1,128)} %broadcast_in_dim.31), calls=%async_computation.7 | async-start | bytes 1581056 | tf_op jit(solution)/shard_map/all_to_all | solution.py:20
  169.8 13.0 %all-to-all-done.7 = f32[8,1,24592]{2,1,0:T(1,128)S(1)} async-done(((f32[8,1,24592]{2,1,0:T(1,128)}), f32[8,1,24592]{2,1,0:T(1,128)S(1)}, u32[]{:S(2)}, u32[]{:S(2)}) %all-to-all-start.7) | async-done | bytes 786976 | tf_op jit(solution)/shard_map/all_to_all | solution.py:20
  186.5 4.1 %all-to-all-start.8 = ((f32[16,1,1]{2,1,0:T(1,128)}), f32[16,1,1]{2,1,0:T(1,128)S(1)}, u32[]{:S(2)}, u32[]{:S(2)}) async-start(f32[16,1,1]{2,1,0:T(1,128)} %broadcast_in_dim.32), calls=%async_computation.8 | async-start | bytes 16384 | tf_op jit(solution)/shard_map/all_to_all | solution.py:20
  190.6 7.0 %all-to-all-done.8 = f32[16,1,1]{2,1,0:T(1,128)S(1)} async-done(((f32[16,1,1]{2,1,0:T(1,128)}), f32[16,1,1]{2,1,0:T(1,128)S(1)}, u32[]{:S(2)}, u32[]{:S(2)}) %all-to-all-start.8) | async-done | bytes 96 | tf_op jit(solution)/shard_map/all_to_all | solution.py:20
  (59 shorter events, 24.4 us)
Async XLA Ops:
  2.9 6.0 %copy-start.4 = (s32[4]{0:T(128)S(1)}, s32[4]{0:T(128)}, u32[]{:S(2)}) copy-start(s32[4]{0:T(128)} %param.10) | copy-start | bytes 52
  2.9 10.5 %copy-start.3 = (s32[4]{0:T(128)S(1)}, s32[4]{0:T(128)}, u32[]{:S(2)}) copy-start(s32[4]{0:T(128)} %param.9) | copy-start | bytes 52
  2.9 14.9 %copy-start.5 = (f32[4,16]{1,0:T(4,128)S(1)}, f32[4,16]{1,0:T(4,128)}, u32[]{:S(2)}) copy-start(f32[4,16]{1,0:T(4,128)} %param.11) | copy-start | bytes 772
  2.9 16.2 %copy-start.1 = (f32[8192]{0:T(1024)S(1)}, f32[8192]{0:T(1024)}, u32[]{:S(2)}) copy-start(f32[8192]{0:T(1024)} %param.14) | copy-start | bytes 98308
  2.9 27.4 %all-to-all-start = ((f32[8,16,3,1024]{3,1,2,0:T(8,128)}), f32[8,16,3,1024]{3,1,2,0:T(8,128)S(1)}, u32[]{:S(2)}, u32[]{:S(2)}) async-start(f32[8,16,3,1024]{3,1,2,0:T(8,128)} %broadcast_in_dim.22), calls=%async_computation | async-start | bytes 3145728 | tf_op jit(solution)/shard_map/all_to_all | solution.py:20
  30.5 0.9 copy-start
  30.5 4.8 %copy-start.6 = (f32[8192]{0:T(1024)S(1)}, f32[8192]{0:T(1024)}, u32[]{:S(2)}) copy-start(f32[8192]{0:T(1024)} %param.13) | copy-start | bytes 98308
  35.4 21.0 %copy-start.2 = (bf16[4,16,256]{2,1,0:T(8,128)(2,1)S(1)}, bf16[4,16,256]{2,1,0:T(8,128)(2,1)}, u32[]{:S(2)}) copy-start(bf16[4,16,256]{2,1,0:T(8,128)(2,1)} %param.8) | copy-start | bytes 98308
  83.2 16.6 %all-to-all-start.3 = ((f32[8,1,24592]{2,1,0:T(1,128)}), f32[8,1,24592]{2,1,0:T(1,128)S(1)}, u32[]{:S(2)}, u32[]{:S(2)}) async-start(f32[8,1,24592]{2,1,0:T(1,128)} %broadcast_in_dim.26), calls=%async_computation.3 | async-start | bytes 1581056 | tf_op jit(solution)/shard_map/all_to_all | solution.py:20
  104.3 11.0 %all-to-all-start.4 = ((f32[16,1,1]{2,1,0:T(1,128)}), f32[16,1,1]{2,1,0:T(1,128)S(1)}, u32[]{:S(2)}, u32[]{:S(2)}) async-start(f32[16,1,1]{2,1,0:T(1,128)} %broadcast_in_dim.27), calls=%async_computation.4 | async-start | bytes 16384 | tf_op jit(solution)/shard_map/all_to_all | solution.py:20
  166.2 16.6 %all-to-all-start.7 = ((f32[8,1,24592]{2,1,0:T(1,128)}), f32[8,1,24592]{2,1,0:T(1,128)S(1)}, u32[]{:S(2)}, u32[]{:S(2)}) async-start(f32[8,1,24592]{2,1,0:T(1,128)} %broadcast_in_dim.31), calls=%async_computation.7 | async-start | bytes 1581056 | tf_op jit(solution)/shard_map/all_to_all | solution.py:20
  186.5 11.0 %all-to-all-start.8 = ((f32[16,1,1]{2,1,0:T(1,128)}), f32[16,1,1]{2,1,0:T(1,128)S(1)}, u32[]{:S(2)}, u32[]{:S(2)}) async-start(f32[16,1,1]{2,1,0:T(1,128)} %broadcast_in_dim.32), calls=%async_computation.8 | async-start | bytes 16384 | tf_op jit(solution)/shard_map/all_to_all | solution.py:20
where the time goes:
time: 201 us; the launch traced here: 200 us
  blocking collectives  51 us (25%)
  waiting for transfers between devices  46.2 us (23%)
  matrix products  35.4 us (18%)
  starting transfers between devices  21.2 us (11%)
  other arithmetic  20.5 us (10%)
  between operations  13.5 us (7%)
  local copies, waits for them, and re-layouts  11.8 us (6%)
    all_to_all x5, waiting for transfers between devices, copy_for_each(): lax.all_to_all(jnp.broadcast_to(value[None], (devices, *value.shape)), ax...  46.2 us
    all_to_all x2, blocking collectives, sum_at_owner(): lax.all_to_all(split_up(value, dim, devices), axis, 0, 0, tiled=True)  28.8 us
    all_to_all x2, blocking collectives, copy_for_each(): lax.all_to_all(jnp.broadcast_to(value[None], (devices, *value.shape)), ax...  22.2 us
    all_to_all x5, starting transfers between devices, copy_for_each(): lax.all_to_all(jnp.broadcast_to(value[None], (devices, *value.shape)), ax...  21.2 us
    dot_general x2, matrix products, body(): lax.dot_general(profile_v, whole_b, (((1,), (1,)), ((), ())), preferred_e...  10.2 us
    dot_general x2, matrix products, body(): weighted_v = jnp.dot(profile_u, whole_b, preferred_element_type=jnp.float32)  10.1 us
    dot_general x2, matrix products, body(): lax.dot_general(profile_u, profile_v, (((0,), (0,)), ((), ())), preferred...  7.93 us
    add x2, other arithmetic, factors(): rotation[1, 0] * positions[0] + rotation[1, 1] * positions[1]  7.67 us
  transfers between devices with their start and end apart: 5, of which 5 were waited for; matrix products, arithmetic and copies ran while one was open for 2% of the time, Pallas kernels for 0%

commit v1 on v0

v1 whole, which is shorter than its diff:
```python
import functools
import math

import jax
import jax.numpy as jnp
from jax import lax
from jax.experimental import pallas as pl
from jax.experimental.pallas import tpu as pltpu
from jax.sharding import PartitionSpec as P

PIX = 256
K = 16
NROT = 4096
STEPS = 2
SUB = 1024
TILES = SUB // 128
BLK = 256
CENTER = (PIX - 1) * 0.5

step_size = 0.5
tiny_eps = 1e-06
MESH = pl.DeviceIdType.MESH
HIGH = lax.Precision.HIGHEST


def cos_sin(units):
    quarter = (
        (units >= 18).astype(jnp.int32)
        + (units >= 54).astype(jnp.int32)
        + (units >= 90).astype(jnp.int32)
        + (units >= 126).astype(jnp.int32)
    )
    x = (units - 36 * quarter).astype(jnp.float32) * (2.0 * math.pi / 144.0)
    y = x * x
    s = x * (1.0 + y * (-1.0 / 6 + y * (1.0 / 120 + y * (-1.0 / 5040 + y * (1.0 / 362880)))))
    c = 1.0 + y * (
        -0.5 + y * (1.0 / 24 + y * (-1.0 / 720 + y * (1.0 / 40320 - y * (1.0 / 3628800))))
    )
    odd = (quarter == 1) | (quarter == 3)
    cos_a = jnp.where(odd, s, c)
    sin_a = jnp.where(odd, c, s)
    cos_a = jnp.where((quarter == 1) | (quarter == 2), -cos_a, cos_a)
    sin_a = jnp.where((quarter == 2) | (quarter == 3), -sin_a, sin_a)
    return cos_a, sin_a


def own_coefficients(pose, latent):
    lane = lax.broadcasted_iota(jnp.int32, (1, 128), 1)
    n = jnp.full((1, 128), pose, jnp.int32)
    cos_b = 1.0 - (2 * n + 1).astype(jnp.float32) * (1.0 / NROT)
    sin_b = jnp.sqrt(1.0 - cos_b * cos_b)
    cos_a, sin_a = cos_sin(jnp.full((1, 128), lax.rem(pose * 55, 144), jnp.int32))
    cos_g, sin_g = cos_sin(jnp.full((1, 128), lax.rem(pose, 8) * 18, jnp.int32))
    rows = (
        (
            cos_a * cos_b * cos_g - sin_a * sin_g,
            -cos_a * cos_b * sin_g - sin_a * cos_g,
            cos_a * sin_b,
        ),
        (
            sin_a * cos_b * cos_g + cos_a * sin_g,
            -sin_a * cos_b * sin_g + cos_a * cos_g,
            sin_a * sin_b,
        ),
    )
    spread = latent + pltpu.roll(latent, K, 1) + pltpu.roll(latent, 2 * K, 1)
    spread = jnp.where(lane < 3 * K, spread, jnp.where(lane < 3 * K + 3, 1.0, 0.0))
    first = (lane < K) | (lane == 3 * K)
    second = ((lane >= K) & (lane < 2 * K)) | (lane == 3 * K + 1)
    return [spread * jnp.where(first, r[0], jnp.where(second, r[1], r[2])) for r in rows]


def kernel(
    ng,
    ni,
    pose_ref,
    order_ref,
    lat_ref,
    obs_hbm,
    base_hbm,
    amp_hbm,
    wid_hbm,
    modes_hbm,
    res_hbm,
    new_hbm,
    zpad,
    obs,
    rows_in,
    base_in,
    amp,
    wid,
    curve,
    psend,
    params,
    xbuf,
    asend,
    arecv,
    bsend,
    brecv,
    proj,
    pu,
    pv,
    image,
    isend,
    irecv,
    resid,
    rsend,
    whole,
    whole_t,
    grads,
    gsend,
    grecv,
    mgrad,
    s1,
    s2send,
    s2,
    newv,
    in_sem,
    out_sem,
    p_sem,
    a_sem,
    b_sem,
    i_sem,
    r_sem,
    g_sem,
    s1_sem,
    s2_sem,
):
    rows = PIX // ng
    blocks = ni * SUB // BLK
    per_sub = SUB // BLK
    entries = 3 * K * SUB * ni * ng
    gj = lax.axis_index("gauss")
    ib = lax.axis_index("img")

    loads = [
        pltpu.make_async_copy(modes_hbm, rows_in.at[pl.ds(0, 3 * K)], in_sem.at[0]),
        pltpu.make_async_copy(
            base_hbm.at[:, pl.ds(pl.multiple_of(ib * SUB, SUB), SUB)], base_in, in_sem.at[1]
        ),
        pltpu.make_async_copy(amp_hbm, amp, in_sem.at[2]),
        pltpu.make_async_copy(wid_hbm, wid, in_sem.at[3]),
        pltpu.make_async_copy(obs_hbm, obs, in_sem.at[4]),
    ]
    for copy in loads:
        copy.start()

    barrier = pltpu.get_barrier_semaphore()
    for axis, me, n in (("img", ib, ni), ("gauss", gj, ng)):
        for r in range(1, n):
            pl.semaphore_signal(
                barrier, inc=1, device_id={axis: lax.rem(me + r, n)}, device_id_type=MESH
            )

    zpad[...] = jnp.zeros_like(zpad)
    zpad[0:4, 0:K] = lat_ref[...]
    chosen = [order_ref[s] for s in range(STEPS)]
    psend[...] = jnp.zeros_like(psend)
    for s in range(STEPS):
        both = own_coefficients(pose_ref[chosen[s]], zpad[pl.ds(chosen[s], 1), :])
        psend[2 * s : 2 * s + 1, :] = both[0]
        psend[2 * s + 1 : 2 * s + 2, :] = both[1]
    params[ib] = psend[...]

    pl.semaphore_wait(barrier, ni + ng - 2)

    def send_all(axis, source, target, sem):
        me, n = (ib, ni) if axis == "img" else (gj, ng)
        for r in range(1, n):
            peer = lax.rem(me + r, n)
            pltpu.make_async_remote_copy(
                src_ref=source(peer),
                dst_ref=target(me, r),
                send_sem=sem.at[0],
                recv_sem=sem.at[1],
                device_id={axis: peer},
                device_id_type=MESH,
            ).start()

    def wait_for(part, sem):
        pltpu.make_async_copy(part, part, sem).wait()

    send_all("img", lambda peer: psend, lambda me, r: params.at[me], p_sem)

    loads[0].wait()
    loads[1].wait()
    rows_in[3 * K :, :] = jnp.zeros_like(rows_in[3 * K :, :])
    rows_in[3 * K : 3 * K + 3, :] = base_in[...]
    loads[3].wait()
    w = wid[...]
    inv = 1.0 / (w * w)
    curve[1] = inv
    curve[0] = inv * (-0.5 * math.log2(math.e))

    wait_for(params.at[pl.ds(0, ni - 1)], p_sem.at[1])

    def coefficients(s):
        return jnp.concatenate([params[:, 2 * s, :], params[:, 2 * s + 1, :]], axis=0)

    def project(s, source, center, target):
        got = lax.dot_general(
            coefficients(s)[:, : source.shape[0]],
            source,
            (((1,), (0,)), ((), ())),
            precision=HIGH,
            preferred_element_type=jnp.float32,
        )
        if center:
            got = got + CENTER
        for t in range(TILES):
            xbuf[t] = got[:, t * 128 : (t + 1) * 128]
        for b in range(ni):
            for uv in range(2):
                target[b, uv] = xbuf[:, uv * ni + b, :]

    project(0, rows_in[...], True, asend.at[0])
    send_all("img", lambda peer: asend.at[0, peer], lambda me, r: arecv.at[0, me], a_sem.at[0])
    arecv[0, ib] = asend[0, ib]
    project(1, rows_in[...], True, asend.at[1])
    send_all("img", lambda peer: asend.at[1, peer], lambda me, r: arecv.at[1, me], a_sem.at[1])
    arecv[1, ib] = asend[1, ib]
    loads[2].wait()
    wait_for(arecv.at[0, pl.ds(0, ni - 1)], a_sem.at[0, 1])

    pixel16 = lax.broadcasted_iota(jnp.int32, (16, 128), 0).astype(jnp.float32)
    halves = []

    for s in range(STEPS):
        if s == 0:
            proj[...] = arecv[0]
        else:
            wait_for(arecv.at[1, pl.ds(0, ni - 1)], a_sem.at[1, 1])
            wait_for(brecv.at[pl.ds(0, ni - 1)], b_sem.at[1])
            proj[...] = arecv[1] - halves[0] * brecv[...]

        image[...] = jnp.zeros_like(image)

        def render(i, carry):
            b = i // per_sub
            t0 = (i % per_sub) * (BLK // 128)
            for tt in range(BLK // 128):
                g = b * TILES + t0 + tt
                c = curve[0, pl.ds(g, 1), :]
                a = amp[pl.ds(g, 1), :]
                lanes = slice(tt * 128, (tt + 1) * 128)
                du = pixel16 - proj[b, 0, pl.ds(t0 + tt, 1), :]
                dv = pixel16 - proj[b, 1, pl.ds(t0 + tt, 1), :]
                for m in range(PIX // 16):
                    d = du + 16.0 * m
                    pu[i, m * 16 : (m + 1) * 16, lanes] = jnp.exp2(d * d * c).astype(jnp.bfloat16)
                    d = dv + 16.0 * m
                    pv[i, m * 16 : (m + 1) * 16, lanes] = (a * jnp.exp2(d * d * c)).astype(
                        jnp.bfloat16
                    )
            image[...] += lax.dot_general(
                pu[i],
                pv[i],
                (((1,), (1,)), ((), ())),
                preferred_element_type=jnp.float32,
            )
            return carry

        lax.fori_loop(0, blocks, render, 0)

        for j in range(ng):
            isend[s, j] = image[j * rows : (j + 1) * rows, :].astype(isend.dtype)
        send_all(
            "gauss",
            lambda peer: isend.at[s, peer],
            lambda me, r: irecv.at[s, r - 1],
            i_sem.at[s],
        )
        if s == 0:
            loads[4].wait()
        measured = obs[chosen[s]].astype(jnp.float32)
        total = image[pl.ds(pl.multiple_of(gj * rows, rows), rows), :] - measured
        wait_for(irecv.at[s], i_sem.at[s, 1])
        for r in range(ng - 1):
            total = total + irecv[s, r].astype(jnp.float32)
        rsend[s] = total.astype(jnp.bfloat16)
        send_all("gauss", lambda peer: rsend.at[s], lambda me, r: whole.at[s, me], r_sem.at[s])
        whole[s, gj] = rsend[s]
        if s == STEPS - 1:
            resid[...] = total
            pltpu.make_async_copy(resid, res_hbm, out_sem.at[0]).start()
        wait_for(whole.at[s, pl.ds(0, ng - 1)], r_sem.at[s, 1])
        whole_t[0] = whole[s].reshape(PIX, PIX)
        whole_t[1] = whole_t[0].T

        def backward(i, carry):
            b = i // per_sub
            t0 = (i % per_sub) * (BLK // 128)
            sides = ((0, pu, whole_t[0], pv), (1, pv, whole_t[1], pu))
            for uv, own, matrix, other in sides:
                weighted = jnp.dot(matrix, other[i], preferred_element_type=jnp.float32)
                for tt in range(BLK // 128):
                    g = b * TILES + t0 + tt
                    lanes = slice(tt * 128, (tt + 1) * 128)
                    d0 = pixel16 - proj[b, uv, pl.ds(t0 + tt, 1), :]
                    total = jnp.zeros((16, 128), jnp.float32)
                    for m in range(PIX // 16):
                        span = slice(m * 16, (m + 1) * 16)
                        total += (
                            own[i, span, lanes].astype(jnp.float32)
                            * (d0 + 16.0 * m)
                            * weighted[span, lanes]
                        )
                    gsend[s, b, uv, pl.ds(t0 + tt, 1), :] = curve[1, pl.ds(g, 1), :] * jnp.sum(
                        total, axis=0, keepdims=True
                    )
            return carry

        lax.fori_loop(0, blocks, backward, 0)

        send_all("img", lambda peer: gsend.at[s, peer], lambda me, r: grecv.at[s, me], g_sem.at[s])
        grecv[s, ib] = gsend[s, ib]
        wait_for(grecv.at[s, pl.ds(0, ni - 1)], g_sem.at[s, 1])
        for uv in range(2):
            for t in range(TILES):
                grads[uv * ni : (uv + 1) * ni, t * 128 : (t + 1) * 128] = grecv[s, :, uv, t, :]
        got = lax.dot_general(
            coefficients(s)[:, : 3 * K],
            grads[...],
            (((0,), (0,)), ((), ())),
            precision=HIGH,
            preferred_element_type=jnp.float32,
        )
        mgrad[s] = got
        squares = jnp.zeros((8, 128), jnp.float32)
        for k in range(3 * K // 8):
            for t in range(TILES):
                part = got[k * 8 : (k + 1) * 8, t * 128 : (t + 1) * 128]
                squares = squares + part * part
        s1[s, ib] = squares
        send_all("img", lambda peer: s1.at[s, ib], lambda me, r: s1.at[s, me], s1_sem.at[s])
        if s == 0:
            project(1, mgrad[0], False, bsend)
            send_all("img", lambda peer: bsend.at[peer], lambda me, r: brecv.at[me], b_sem)
            brecv[ib] = bsend[ib]
        wait_for(s1.at[s, pl.ds(0, ni - 1)], s1_sem.at[s, 1])
        s2[s, gj] = jnp.sum(s1[s], axis=0)
        send_all("gauss", lambda peer: s2.at[s, gj], lambda me, r: s2.at[s, me], s2_sem.at[s])
        wait_for(s2.at[s, pl.ds(0, ng - 1)], s2_sem.at[s, 1])
        sums = jnp.sum(s2[s], axis=0)
        sums = jnp.sum(jnp.sum(sums, axis=0, keepdims=True), axis=1, keepdims=True)
        halves.append(step_size / jnp.sqrt(sums * (1.0 / entries) + tiny_eps))

    newv[...] = rows_in[: 3 * K, :] - halves[0] * mgrad[0] - halves[1] * mgrad[1]
    done = pltpu.make_async_copy(newv, new_hbm, out_sem.at[1])
    done.start()

    wait_for(params.at[pl.ds(0, ni - 1)], p_sem.at[0])
    wait_for(brecv.at[pl.ds(0, ni - 1)], b_sem.at[0])
    for s in range(STEPS):
        wait_for(arecv.at[s, pl.ds(0, ni - 1)], a_sem.at[s, 0])
        wait_for(irecv.at[s], i_sem.at[s, 0])
        wait_for(whole.at[s, pl.ds(0, ng - 1)], r_sem.at[s, 0])
        wait_for(grecv.at[s, pl.ds(0, ni - 1)], g_sem.at[s, 0])
        wait_for(s1.at[s, pl.ds(0, ni - 1)], s1_sem.at[s, 0])
        wait_for(s2.at[s, pl.ds(0, ng - 1)], s2_sem.at[s, 0])
    pltpu.make_async_copy(resid, res_hbm, out_sem.at[0]).wait()
    done.wait()


def body(
    observed, pose_index, batch_order, latents, base_positions, amplitudes, widths, deform_modes
):
    ng, ni = lax.axis_size("gauss"), lax.axis_size("img")
    rows = PIX // ng
    count = ni * SUB
    blocks = count // BLK
    f32, b16 = jnp.float32, jnp.bfloat16
    vmem, hbm, smem = (
        pl.BlockSpec(memory_space=m) for m in (pltpu.VMEM, pl.ANY, pltpu.SMEM)
    )
    dma = pltpu.SemaphoreType.DMA
    final, new = pl.pallas_call(
        functools.partial(kernel, ng, ni),
        out_shape=(
            jax.ShapeDtypeStruct((rows, PIX), f32),
            jax.ShapeDtypeStruct((3 * K, SUB), f32),
        ),
        in_specs=[smem, smem, vmem, hbm, hbm, hbm, hbm, hbm],
        out_specs=(hbm, hbm),
        scratch_shapes=[
            pltpu.VMEM((8, 128), f32),
            pltpu.VMEM((4, rows, PIX), b16),
            pltpu.VMEM((3 * K + 8, SUB), f32),
            pltpu.VMEM((3, SUB), f32),
            pltpu.VMEM((count // 128, 128), f32),
            pltpu.VMEM((count // 128, 128), f32),
            pltpu.VMEM((2, count // 128, 128), f32),
            pltpu.VMEM((8, 128), f32),
            pltpu.VMEM((ni, 8, 128), f32),
            pltpu.VMEM((TILES, 2 * ni, 128), f32),
            pltpu.VMEM((STEPS, ni, 2, TILES, 128), f32),
            pltpu.VMEM((STEPS, ni, 2, TILES, 128), f32),
            pltpu.VMEM((ni, 2, TILES, 128), f32),
            pltpu.VMEM((ni, 2, TILES, 128), f32),
            pltpu.VMEM((ni, 2, TILES, 128), f32),
            pltpu.VMEM((blocks, PIX, BLK), b16),
            pltpu.VMEM((blocks, PIX, BLK), b16),
            pltpu.VMEM((PIX, PIX), f32),
            pltpu.VMEM((STEPS, ng, rows, PIX), b16),
            pltpu.VMEM((STEPS, ng - 1, rows, PIX), b16),
            pltpu.VMEM((rows, PIX), f32),
            pltpu.VMEM((STEPS, rows, PIX), b16),
            pltpu.VMEM((STEPS, ng, rows, PIX), b16),
            pltpu.VMEM((2, PIX, PIX), b16),
            pltpu.VMEM((2 * ni, SUB), f32),
            pltpu.VMEM((STEPS, ni, 2, TILES, 128), f32),
            pltpu.VMEM((STEPS, ni, 2, TILES, 128), f32),
            pltpu.VMEM((STEPS, 3 * K, SUB), f32),
            pltpu.VMEM((STEPS, ni, 8, 128), f32),
            pltpu.VMEM((8, 128), f32),
            pltpu.VMEM((STEPS, ng, 8, 128), f32),
            pltpu.VMEM((3 * K, SUB), f32),
            dma((5,)),
            dma((2,)),
            dma((2,)),
            dma((STEPS, 2)),
            dma((2,)),
            dma((STEPS, 2)),
            dma((STEPS, 2)),
            dma((STEPS, 2)),
            dma((STEPS, 2)),
            dma((STEPS, 2)),
        ],
        compiler_params=pltpu.CompilerParams(
            collective_id=0, has_side_effects=True, vmem_limit_bytes=48 * 2**20
        ),
    )(
        pose_index,
        batch_order,
        latents,
        observed,
        base_positions,
        amplitudes.reshape(count // 128, 128),
        widths.reshape(count // 128, 128),
        deform_modes.transpose(1, 0, 2).reshape(3 * K, SUB),
    )
    return final[None], new.reshape(3, K, SUB).transpose(1, 0, 2)


def solution(mesh):
    return jax.shard_map(
        body,
        mesh=mesh,
        in_specs=(
            P("img", "gauss", None),
            P("img"),
            P("img"),
            P("img", None),
            P(None, "gauss"),
            P("gauss"),
            P("gauss"),
            P(None, None, ("gauss", "img")),
        ),
        out_specs=(P("img", "gauss", None), P(None, None, ("gauss", "img"))),
        check_vma=False,
    )
```

time: 201 us -> 104 us (0.52)
  Pallas kernels: 0 us -> 97.3 us
  blocking collectives: 51 us -> 0 us
  waiting for transfers between devices: 46.2 us -> 0 us
  matrix products: 35.4 us -> 0 us
  starting transfers between devices: 21.2 us -> 0 us
  other arithmetic: 20.5 us -> 0 us
  between operations: 13.5 us -> 0.67 us
  local copies, waits for them, and re-layouts: 11.8 us -> 6.05 us
    pallas_call x0 -> x1, Pallas kernels: none -> 97.3 us  [body(): pl.pallas_call(functools.partial(kernel, ng, ni), out_shape=(jax.ShapeDty...]
    all_to_all x4 -> x0, blocking collectives: 51 us -> none  [the longest x2 28.8 us: sum_at_owner(): lax.all_to_all(split_up(value, dim, devices), axis, 0, 0, tiled=True)]
    all_to_all x5 -> x0, waiting for transfers between devices: 46.2 us -> none  [copy_for_each(): lax.all_to_all(jnp.broadcast_to(value[None], (devices, *value.shape)), ax...]
    dot_general x10 -> x0, matrix products: 35.4 us -> none  [the longest x2 10.2 us: body(): lax.dot_general(profile_v, whole_b, (((1,), (1,)), ((), ())), preferred_e...]
    all_to_all x5 -> x0, starting transfers between devices: 21.2 us -> none  [copy_for_each(): lax.all_to_all(jnp.broadcast_to(value[None], (devices, *value.shape)), ax...]
    add x6 -> x0, other arithmetic: 15.3 us -> none  [the longest x2 7.67 us: factors(): rotation[1, 0] * positions[0] + rotation[1, 1] * positions[1]]
    broadcast_in_dim x7 -> x0, local copies, waits for them, and re-layouts: 7.39 us -> none  [copy_for_each(): jnp.broadcast_to(value[None], (devices, *value.shape))]
    unnamed x18, local copies, waits for them, and re-layouts: 0.36 us -> 6.05 us
  transfers between devices with their start and end apart: 5 -> 0, of which waited for: 5 -> 0; matrix products, arithmetic and copies ran while one was open for 2% -> 0% of each run, Pallas kernels for 0% -> 0%
where the time goes in v1:
time: 104 us
  Pallas kernels  97.3 us (94%)
  local copies, waits for them, and re-layouts  6.05 us (6%)
    pallas_call x1, Pallas kernels, body(): pl.pallas_call(functools.partial(kernel, ng, ni), out_shape=(jax.ShapeDty...  97.3 us
    unnamed x18, local copies, waits for them, and re-layouts  6.05 us

profile of v1, /device:TPU:1, one launch (start us, length us, event | category | flops | bytes accessed | tf_op | source)
XLA Modules:
  0.0 104.1 jit_solution(4464712241094498)
XLA Ops:
  0.6 0.0 copy-start.5
  0.6 0.0 copy-start.6
  0.7 0.0 copy-start.7
  0.7 0.7 copy-done.5
  1.3 0.0 copy-done.6
  1.3 0.0 copy-done.7
  1.3 0.0 copy-start
  1.3 0.9 copy-done
  2.2 0.0 copy-start.1
  2.3 0.9 copy-done.1
  3.2 0.0 copy-start.2
  3.2 0.8 copy-done.2
  3.9 0.0 copy-start.3
  3.9 0.8 copy-done.3
  4.7 0.0 copy-start.4
  4.7 0.8 copy-done.4
  5.4 97.3 %shard_map.95 = (f32[16,256]{1,0:T(8,128)S(1)}, f32[48,1024]{1,0:T(8,128)S(1)}) custom-call(s32[4]{0:T(128)S(1)} %copy-done.6, s32[4]{0:T(128)S(1)} %copy-done.7, f32[4,16]{1,0:T(4,128)S(1)} %copy-done.5, bf16[4,16,256]{2,1,0:T(8,128)(2,1)S(1)} %copy-done.2, f32[3,8192]{1,0:T(4,128)S(1)} %copy-done.1, f32[64,128]{1,0:T(8,128)S(1)} %bitcast.11, ...), custom_call_target="tpu_custom_call" | custom-call | tf_op jit(solution)/shard_map/pallas_call | solution.py:377
  102.8 0.6 copy.12
  103.4 0.7 copy.13
Async XLA Ops:
  0.6 0.7 copy-start.5
  0.6 0.7 copy-start.6
  0.7 0.7 copy-start.7
  1.3 0.9 copy-start
  2.2 0.9 copy-start.1
  3.2 0.8 copy-start.2
  3.9 0.8 copy-start.3
  4.7 0.8 copy-start.4

commit v2 on v1

--- a/solution.py
+++ b/solution.py
@@ -14,7 +14,7 @@
 STEPS = 2
 SUB = 1024
 TILES = SUB // 128
-BLK = 256
+BLK = 512
 CENTER = (PIX - 1) * 0.5
 
 step_size = 0.5
@@ -95,11 +95,15 @@
     xbuf,
     asend,
     arecv,
-    bsend,
-    brecv,
+    shift,
+    weights,
+    wmat,
     proj,
-    pu,
-    pv,
+    pixels,
+    pu0,
+    pu1,
+    pv0,
+    pv1,
     image,
     isend,
     irecv,
@@ -108,27 +112,27 @@
     whole,
     whole_t,
     grads,
+    gown,
     gsend,
     grecv,
+    gall,
+    gpart,
     mgrad,
-    s1,
-    s2send,
     s2,
     newv,
     in_sem,
     out_sem,
     p_sem,
     a_sem,
-    b_sem,
     i_sem,
     r_sem,
     g_sem,
-    s1_sem,
     s2_sem,
 ):
     rows = PIX // ng
-    blocks = ni * SUB // BLK
-    per_sub = SUB // BLK
+    pairs = ni * SUB // BLK // 2
+    tiles = ni * TILES
+    pus, pvs = (pu0, pu1), (pv0, pv1)
     entries = 3 * K * SUB * ni * ng
     gj = lax.axis_index("gauss")
     ib = lax.axis_index("img")
@@ -145,11 +149,15 @@
     for copy in loads:
         copy.start()
 
+    def partner(axis, n, r):
+        me = ib if axis == "img" else gj
+        return lax.rem(me + (n // 2 + r if r < n // 2 else n - r), n)
+
     barrier = pltpu.get_barrier_semaphore()
-    for axis, me, n in (("img", ib, ni), ("gauss", gj, ng)):
+    for axis, n in (("gauss", ng), ("img", ni)):
         for r in range(1, n):
             pl.semaphore_signal(
-                barrier, inc=1, device_id={axis: lax.rem(me + r, n)}, device_id_type=MESH
+                barrier, inc=1, device_id={axis: partner(axis, n, r)}, device_id_type=MESH
             )
 
     zpad[...] = jnp.zeros_like(zpad)
@@ -167,7 +175,7 @@
     def send_all(axis, source, target, sem):
         me, n = (ib, ni) if axis == "img" else (gj, ng)
         for r in range(1, n):
-            peer = lax.rem(me + r, n)
+            peer = partner(axis, n, r)
             pltpu.make_async_remote_copy(
                 src_ref=source(peer),
                 dst_ref=target(me, r),
@@ -182,6 +190,7 @@
 
     send_all("img", lambda peer: psend, lambda me, r: params.at[me], p_sem)
 
+    pixels[...] = lax.broadcasted_iota(jnp.int32, (PIX, 128), 0).astype(jnp.float32)
     loads[0].wait()
     loads[1].wait()
     rows_in[3 * K :, :] = jnp.zeros_like(rows_in[3 * K :, :])
@@ -197,32 +206,30 @@
     def coefficients(s):
         return jnp.concatenate([params[:, 2 * s, :], params[:, 2 * s + 1, :]], axis=0)
 
-    def project(s, source, center, target):
+    def project(s):
         got = lax.dot_general(
-            coefficients(s)[:, : source.shape[0]],
-            source,
+            coefficients(s)[:, : 3 * K + 8],
+            rows_in[...],
             (((1,), (0,)), ((), ())),
             precision=HIGH,
             preferred_element_type=jnp.float32,
         )
-        if center:
-            got = got + CENTER
+        got = got + CENTER
         for t in range(TILES):
             xbuf[t] = got[:, t * 128 : (t + 1) * 128]
         for b in range(ni):
             for uv in range(2):
-                target[b, uv] = xbuf[:, uv * ni + b, :]
-
-    project(0, rows_in[...], True, asend.at[0])
+                asend[s, b, uv] = xbuf[:, uv * ni + b, :]
+
+    project(0)
     send_all("img", lambda peer: asend.at[0, peer], lambda me, r: arecv.at[0, me], a_sem.at[0])
     arecv[0, ib] = asend[0, ib]
-    project(1, rows_in[...], True, asend.at[1])
+    project(1)
     send_all("img", lambda peer: asend.at[1, peer], lambda me, r: arecv.at[1, me], a_sem.at[1])
     arecv[1, ib] = asend[1, ib]
     loads[2].wait()
     wait_for(arecv.at[0, pl.ds(0, ni - 1)], a_sem.at[0, 1])
 
-    pixel16 = lax.broadcasted_iota(jnp.int32, (16, 128), 0).astype(jnp.float32)
     halves = []
 
     for s in range(STEPS):
@@ -230,37 +237,43 @@
             proj[...] = arecv[0]
         else:
             wait_for(arecv.at[1, pl.ds(0, ni - 1)], a_sem.at[1, 1])
-            wait_for(brecv.at[pl.ds(0, ni - 1)], b_sem.at[1])
-            proj[...] = arecv[1] - halves[0] * brecv[...]
+            proj[...] = arecv[1] - halves[0] * shift[...]
 
         image[...] = jnp.zeros_like(image)
 
-        def render(i, carry):
-            b = i // per_sub
-            t0 = (i % per_sub) * (BLK // 128)
-            for tt in range(BLK // 128):
-                g = b * TILES + t0 + tt
+        def profiles(half, j):
+            for t in range(BLK // 128):
+                g = (2 * j + half) * (BLK // 128) + t
+                b, row = g // TILES, g % TILES
                 c = curve[0, pl.ds(g, 1), :]
-                a = amp[pl.ds(g, 1), :]
-                lanes = slice(tt * 128, (tt + 1) * 128)
-                du = pixel16 - proj[b, 0, pl.ds(t0 + tt, 1), :]
-                dv = pixel16 - proj[b, 1, pl.ds(t0 + tt, 1), :]
-                for m in range(PIX // 16):
-                    d = du + 16.0 * m
-                    pu[i, m * 16 : (m + 1) * 16, lanes] = jnp.exp2(d * d * c).astype(jnp.bfloat16)
-                    d = dv + 16.0 * m
-                    pv[i, m * 16 : (m + 1) * 16, lanes] = (a * jnp.exp2(d * d * c)).astype(
-                        jnp.bfloat16
-                    )
+                lanes = slice(t * 128, (t + 1) * 128)
+                d = pixels[...] - proj[b, 0, pl.ds(row, 1), :]
+                pus[half][j, :, lanes] = jnp.exp2(d * d * c).astype(jnp.bfloat16)
+                d = pixels[...] - proj[b, 1, pl.ds(row, 1), :]
+                pvs[half][j, :, lanes] = (amp[pl.ds(g, 1), :] * jnp.exp2(d * d * c)).astype(
+                    jnp.bfloat16
+                )
+
+        def add_image(half, j):
             image[...] += lax.dot_general(
-                pu[i],
-                pv[i],
+                pus[half][j],
+                pvs[half][j],
                 (((1,), (1,)), ((), ())),
                 preferred_element_type=jnp.float32,
             )
+
+        def render(j, carry):
+            add_image(0, j - 1)
+            profiles(1, j - 1)
+            add_image(1, j - 1)
+            profiles(0, j)
             return carry
 
-        lax.fori_loop(0, blocks, render, 0)
+        profiles(0, 0)
+        lax.fori_loop(1, pairs, render, 0)
+        add_image(0, pairs - 1)
+        profiles(1, pairs - 1)
+        add_image(1, pairs - 1)
 
         for j in range(ng):
             isend[s, j] = image[j * rows : (j + 1) * rows, :].astype(isend.dtype)
@@ -274,6 +287,26 @@
             loads[4].wait()
         measured = obs[chosen[s]].astype(jnp.float32)
         total = image[pl.ds(pl.multiple_of(gj * rows, rows), rows), :] - measured
+        cross = coefficients(s)[:, : 3 * K]
+        other = jnp.concatenate([cross, psend[:, : 3 * K]], axis=0)
+        wmat[...] = lax.dot_general(
+            other,
+            cross,
+            (((1,), (1,)), ((), ())),
+            precision=HIGH,
+            preferred_element_type=jnp.float32,
+        )
+        for i in range(2 * ni):
+            for k in range(i, 2 * ni):
+                factor = 1.0 if i == k else 2.0
+                weights[i, k] = jnp.broadcast_to(factor * wmat[i : i + 1, k : k + 1], (8, 128))
+        if s == 0:
+            for i in range(2 * ni):
+                for uv in range(2):
+                    at = 2 * ni + 2 + uv
+                    weights[2 * ni + uv, i] = jnp.broadcast_to(
+                        wmat[at : at + 1, i : i + 1], (8, 128)
+                    )
         wait_for(irecv.at[s], i_sem.at[s, 1])
         for r in range(ng - 1):
             total = total + irecv[s, r].astype(jnp.float32)
@@ -287,76 +320,78 @@
         whole_t[0] = whole[s].reshape(PIX, PIX)
         whole_t[1] = whole_t[0].T
 
-        def backward(i, carry):
-            b = i // per_sub
-            t0 = (i % per_sub) * (BLK // 128)
-            sides = ((0, pu, whole_t[0], pv), (1, pv, whole_t[1], pu))
-            for uv, own, matrix, other in sides:
-                weighted = jnp.dot(matrix, other[i], preferred_element_type=jnp.float32)
-                for tt in range(BLK // 128):
-                    g = b * TILES + t0 + tt
-                    lanes = slice(tt * 128, (tt + 1) * 128)
-                    d0 = pixel16 - proj[b, uv, pl.ds(t0 + tt, 1), :]
-                    total = jnp.zeros((16, 128), jnp.float32)
-                    for m in range(PIX // 16):
-                        span = slice(m * 16, (m + 1) * 16)
-                        total += (
-                            own[i, span, lanes].astype(jnp.float32)
-                            * (d0 + 16.0 * m)
-                            * weighted[span, lanes]
+        def backward(j, carry):
+            for half in range(2):
+                sides = ((0, pus, whole_t[0], pvs), (1, pvs, whole_t[1], pus))
+                for uv, own, matrix, other in sides:
+                    weighted = jnp.dot(matrix, other[half][j], preferred_element_type=jnp.float32)
+                    for t in range(BLK // 128):
+                        g = (2 * j + half) * (BLK // 128) + t
+                        b, row = g // TILES, g % TILES
+                        lanes = slice(t * 128, (t + 1) * 128)
+                        d = pixels[...] - proj[b, uv, pl.ds(row, 1), :]
+                        total = own[half][j, :, lanes].astype(jnp.float32) * d * weighted[:, lanes]
+                        gown[pl.ds(uv * tiles + g, 1), :] = curve[1, pl.ds(g, 1), :] * jnp.sum(
+                            total, axis=0, keepdims=True
                         )
-                    gsend[s, b, uv, pl.ds(t0 + tt, 1), :] = curve[1, pl.ds(g, 1), :] * jnp.sum(
-                        total, axis=0, keepdims=True
-                    )
             return carry
 
-        lax.fori_loop(0, blocks, backward, 0)
-
-        send_all("img", lambda peer: gsend.at[s, peer], lambda me, r: grecv.at[s, me], g_sem.at[s])
-        grecv[s, ib] = gsend[s, ib]
+        lax.fori_loop(0, pairs, backward, 0)
+
+        gsend[s] = gown[...].astype(jnp.bfloat16)
+        send_all("img", lambda peer: gsend.at[s], lambda me, r: grecv.at[s, me], g_sem.at[s])
+        grecv[s, ib] = gsend[s]
         wait_for(grecv.at[s, pl.ds(0, ni - 1)], g_sem.at[s, 1])
+        gall[...] = grecv[s].astype(jnp.float32)
+
+        def gradient(i):
+            return gall[i % ni, (i // ni) * tiles : (i // ni + 1) * tiles, :]
+
+        squares = jnp.zeros((8, 128), jnp.float32)
+        for i in range(2 * ni):
+            gi = gradient(i)
+            for k in range(i, 2 * ni):
+                product = (gi * gradient(k)).reshape(tiles // 8, 8, 128)
+                squares = squares + weights[i, k] * jnp.sum(product, axis=0)
+        s2[s, gj] = squares
+        send_all("gauss", lambda peer: s2.at[s, gj], lambda me, r: s2.at[s, me], s2_sem.at[s])
+        if s == 0:
+            for uv in range(2):
+                moved = jnp.zeros((ni, TILES, 128), jnp.float32)
+                for i in range(2 * ni):
+                    moved = moved + weights[2 * ni + uv, i] * gradient(i).reshape(ni, TILES, 128)
+                shift[:, uv] = moved
+        for b in range(ni):
+            for uv in range(2):
+                first = pl.multiple_of(uv * tiles + ib * TILES, TILES)
+                gpart[b, uv] = gall[b, pl.ds(first, TILES), :]
         for uv in range(2):
             for t in range(TILES):
-                grads[uv * ni : (uv + 1) * ni, t * 128 : (t + 1) * 128] = grecv[s, :, uv, t, :]
-        got = lax.dot_general(
+                grads[uv * ni : (uv + 1) * ni, t * 128 : (t + 1) * 128] = gpart[:, uv, t, :]
+        mgrad[s] = lax.dot_general(
             coefficients(s)[:, : 3 * K],
             grads[...],
             (((0,), (0,)), ((), ())),
             precision=HIGH,
             preferred_element_type=jnp.float32,
         )
-        mgrad[s] = got
-        squares = jnp.zeros((8, 128), jnp.float32)
-        for k in range(3 * K // 8):
-            for t in range(TILES):
-                part = got[k * 8 : (k + 1) * 8, t * 128 : (t + 1) * 128]
-                squares = squares + part * part
-        s1[s, ib] = squares
-        send_all("img", lambda peer: s1.at[s, ib], lambda me, r: s1.at[s, me], s1_sem.at[s])
-        if s == 0:
-            project(1, mgrad[0], False, bsend)
-            send_all("img", lambda peer: bsend.at[peer], lambda me, r: brecv.at[me], b_sem)
-            brecv[ib] = bsend[ib]
-        wait_for(s1.at[s, pl.ds(0, ni - 1)], s1_sem.at[s, 1])
-        s2[s, gj] = jnp.sum(s1[s], axis=0)
-        send_all("gauss", lambda peer: s2.at[s, gj], lambda me, r: s2.at[s, me], s2_sem.at[s])
+        if s == 1:
+            newv[...] = rows_in[: 3 * K, :] - halves[0] * mgrad[0]
         wait_for(s2.at[s, pl.ds(0, ng - 1)], s2_sem.at[s, 1])
         sums = jnp.sum(s2[s], axis=0)
         sums = jnp.sum(jnp.sum(sums, axis=0, keepdims=True), axis=1, keepdims=True)
         halves.append(step_size / jnp.sqrt(sums * (1.0 / entries) + tiny_eps))
 
-    newv[...] = rows_in[: 3 * K, :] - halves[0] * mgrad[0] - halves[1] * mgrad[1]
+    newv[...] = newv[...] - halves[1] * mgrad[1]
     done = pltpu.make_async_copy(newv, new_hbm, out_sem.at[1])
     done.start()
 
     wait_for(params.at[pl.ds(0, ni - 1)], p_sem.at[0])
-    wait_for(brecv.at[pl.ds(0, ni - 1)], b_sem.at[0])
     for s in range(STEPS):
         wait_for(arecv.at[s, pl.ds(0, ni - 1)], a_sem.at[s, 0])
         wait_for(irecv.at[s], i_sem.at[s, 0])
         wait_for(whole.at[s, pl.ds(0, ng - 1)], r_sem.at[s, 0])
         wait_for(grecv.at[s, pl.ds(0, ni - 1)], g_sem.at[s, 0])
-        wait_for(s1.at[s, pl.ds(0, ni - 1)], s1_sem.at[s, 0])
         wait_for(s2.at[s, pl.ds(0, ng - 1)], s2_sem.at[s, 0])
     pltpu.make_async_copy(resid, res_hbm, out_sem.at[0]).wait()
     done.wait()
@@ -368,7 +403,7 @@
     ng, ni = lax.axis_size("gauss"), lax.axis_size("img")
     rows = PIX // ng
     count = ni * SUB
-    blocks = count // BLK
+    pairs = count // BLK // 2
     f32, b16 = jnp.float32, jnp.bfloat16
     vmem, hbm, smem = (
         pl.BlockSpec(memory_space=m) for m in (pltpu.VMEM, pl.ANY, pltpu.SMEM)
@@ -396,10 +431,14 @@
             pltpu.VMEM((STEPS, ni, 2, TILES, 128), f32),
             pltpu.VMEM((STEPS, ni, 2, TILES, 128), f32),
             pltpu.VMEM((ni, 2, TILES, 128), f32),
+            pltpu.VMEM((2 * ni + 2, 2 * ni, 8, 128), f32),
+            pltpu.VMEM((2 * ni + 8, 2 * ni), f32),
             pltpu.VMEM((ni, 2, TILES, 128), f32),
-            pltpu.VMEM((ni, 2, TILES, 128), f32),
-            pltpu.VMEM((blocks, PIX, BLK), b16),
-            pltpu.VMEM((blocks, PIX, BLK), b16),
+            pltpu.VMEM((PIX, 128), f32),
+            pltpu.VMEM((pairs, PIX, BLK), b16),
+            pltpu.VMEM((pairs, PIX, BLK), b16),
+            pltpu.VMEM((pairs, PIX, BLK), b16),
+            pltpu.VMEM((pairs, PIX, BLK), b16),
             pltpu.VMEM((PIX, PIX), f32),
             pltpu.VMEM((STEPS, ng, rows, PIX), b16),
             pltpu.VMEM((STEPS, ng - 1, rows, PIX), b16),
@@ -408,17 +447,16 @@
             pltpu.VMEM((STEPS, ng, rows, PIX), b16),
             pltpu.VMEM((2, PIX, PIX), b16),
             pltpu.VMEM((2 * ni, SUB), f32),
-            pltpu.VMEM((STEPS, ni, 2, TILES, 128), f32),
-            pltpu.VMEM((STEPS, ni, 2, TILES, 128), f32),
+            pltpu.VMEM((2 * count // 128, 128), f32),
+            pltpu.VMEM((STEPS, 2 * count // 128, 128), b16),
+            pltpu.VMEM((STEPS, ni, 2 * count // 128, 128), b16),
+            pltpu.VMEM((ni, 2 * count // 128, 128), f32),
+            pltpu.VMEM((ni, 2, TILES, 128), f32),
             pltpu.VMEM((STEPS, 3 * K, SUB), f32),
-            pltpu.VMEM((STEPS, ni, 8, 128), f32),
-            pltpu.VMEM((8, 128), f32),
             pltpu.VMEM((STEPS, ng, 8, 128), f32),
             pltpu.VMEM((3 * K, SUB), f32),
             dma((5,)),
             dma((2,)),
-            dma((2,)),
-            dma((STEPS, 2)),
             dma((2,)),
             dma((STEPS, 2)),
             dma((STEPS, 2)),
@@ -427,7 +465,7 @@
             dma((STEPS, 2)),
         ],
         compiler_params=pltpu.CompilerParams(
-            collective_id=0, has_side_effects=True, vmem_limit_bytes=48 * 2**20
+            collective_id=0, has_side_effects=True, vmem_limit_bytes=60 * 2**20
         ),
     )(
         pose_index,

time: 104 us -> 83.8 us (0.81)
  Pallas kernels: 97.3 us -> 80 us
  local copies, waits for them, and re-layouts: 6.05 us -> 2.94 us
    pallas_call x1, Pallas kernels: 97.3 us -> 80 us  [body(): pl.pallas_call(functools.partial(kernel, ng, ni), out_shape=(jax.ShapeDty...]
    unnamed x18 -> x2, local copies, waits for them, and re-layouts: 6.05 us -> 2.94 us
where the time goes in v2:
time: 83.8 us; the launch traced here: 83.6 us
  Pallas kernels  80 us (95%)
  local copies, waits for them, and re-layouts  2.94 us (4%)
    pallas_call x1, Pallas kernels, body(): pl.pallas_call(functools.partial(kernel, ng, ni), out_shape=(jax.ShapeDty...  80 us
    unnamed x2, local copies, waits for them, and re-layouts  2.94 us

profile of v2, /device:TPU:1, one launch (start us, length us, event | category | flops | bytes accessed | tf_op | source)
XLA Modules:
  0.0 83.6 jit_solution(3363251040218674111)
XLA Ops:
  0.6 80.0 %shard_map.95 = (f32[16,256]{1,0:T(8,128)}, f32[48,1024]{1,0:T(8,128)}) custom-call(s32[4]{0:T(128)} %pose_ref.1, s32[4]{0:T(128)} %order_ref.1, f32[4,16]{1,0:T(4,128)} %lat_ref.1, bf16[4,16,256]{2,1,0:T(8,128)(2,1)} %obs_hbm.1, f32[3,8192]{1,0:T(4,128)} %base_hbm.1, f32[64,128]{1,0:T(8,128)} %bitcast.11, f32[64,128]{1,0:T(8,128)} %bitcast.12, ...), custom_call_target="tpu_custom_call" | custom-call | tf_op jit(solution)/shard_map/pallas_call | solution.py:412
  80.6 1.3 %copy.12 = f32[1,16,256]{2,1,0:T(8,128)} copy(f32[1,16,256]{2,1,0:T(8,128)} %bitcast.13) | data formatting | bytes 32768
  81.9 1.6 %copy.13 = f32[16,3,1024]{2,0,1:T(8,128)} copy(f32[16,3,1024]{2,0,1:T(8,128)} %bitcast.9) | data formatting | bytes 393216

commit v3 on v2

--- a/solution.py
+++ b/solution.py
@@ -14,6 +14,9 @@
 STEPS = 2
 SUB = 1024
 TILES = SUB // 128
+CHUNK = 2048
+SUBS = CHUNK // SUB
+CTILES = CHUNK // 128
 BLK = 512
 CENTER = (PIX - 1) * 0.5
 
@@ -100,10 +103,8 @@
     wmat,
     proj,
     pixels,
-    pu0,
-    pu1,
-    pv0,
-    pv1,
+    pu,
+    pv,
     image,
     isend,
     irecv,
@@ -130,9 +131,7 @@
     s2_sem,
 ):
     rows = PIX // ng
-    pairs = ni * SUB // BLK // 2
-    tiles = ni * TILES
-    pus, pvs = (pu0, pu1), (pv0, pv1)
+    chunks = ni * SUB // CHUNK
     entries = 3 * K * SUB * ni * ng
     gj = lax.axis_index("gauss")
     ib = lax.axis_index("img")
@@ -228,52 +227,53 @@
     send_all("img", lambda peer: asend.at[1, peer], lambda me, r: arecv.at[1, me], a_sem.at[1])
     arecv[1, ib] = asend[1, ib]
     loads[2].wait()
-    wait_for(arecv.at[0, pl.ds(0, ni - 1)], a_sem.at[0, 1])
-
     halves = []
 
     for s in range(STEPS):
+        def profiles(b):
+            for t in range(TILES):
+                g = b * TILES + t
+                c = curve[0, pl.ds(g, 1), :]
+                first = pl.multiple_of((b % SUBS) * SUB + t * 128, 128)
+                d = pixels[...] - proj[b, 0, t : t + 1, :]
+                pu[b // SUBS, :, pl.ds(first, 128)] = jnp.exp2(d * d * c).astype(jnp.bfloat16)
+                d = pixels[...] - proj[b, 1, t : t + 1, :]
+                pv[b // SUBS, :, pl.ds(first, 128)] = (
+                    amp[pl.ds(g, 1), :] * jnp.exp2(d * d * c)
+                ).astype(jnp.bfloat16)
+
         if s == 0:
+            proj[ib] = arecv[0, ib]
+            profiles(ib)
+            wait_for(arecv.at[0, pl.ds(0, ni - 1)], a_sem.at[0, 1])
             proj[...] = arecv[0]
         else:
             wait_for(arecv.at[1, pl.ds(0, ni - 1)], a_sem.at[1, 1])
             proj[...] = arecv[1] - halves[0] * shift[...]
 
+        def render(i, carry):
+            profiles(lax.rem(ib + i, ni))
+            return carry
+
+        lax.fori_loop(1 if s == 0 else 0, ni, render, 0)
+
         image[...] = jnp.zeros_like(image)
-
-        def profiles(half, j):
-            for t in range(BLK // 128):
-                g = (2 * j + half) * (BLK // 128) + t
-                b, row = g // TILES, g % TILES
-                c = curve[0, pl.ds(g, 1), :]
-                lanes = slice(t * 128, (t + 1) * 128)
-                d = pixels[...] - proj[b, 0, pl.ds(row, 1), :]
-                pus[half][j, :, lanes] = jnp.exp2(d * d * c).astype(jnp.bfloat16)
-                d = pixels[...] - proj[b, 1, pl.ds(row, 1), :]
-                pvs[half][j, :, lanes] = (amp[pl.ds(g, 1), :] * jnp.exp2(d * d * c)).astype(
-                    jnp.bfloat16
+        together = 2 if chunks % 2 == 0 else 1
+
+        def add_image(i, carry):
+            terms = [
+                lax.dot_general(
+                    pu[i * together + k],
+                    pv[i * together + k],
+                    (((1,), (1,)), ((), ())),
+                    preferred_element_type=jnp.float32,
                 )
-
-        def add_image(half, j):
-            image[...] += lax.dot_general(
-                pus[half][j],
-                pvs[half][j],
-                (((1,), (1,)), ((), ())),
-                preferred_element_type=jnp.float32,
-            )
-
-        def render(j, carry):
-            add_image(0, j - 1)
-            profiles(1, j - 1)
-            add_image(1, j - 1)
-            profiles(0, j)
+                for k in range(together)
+            ]
+            image[...] += sum(terms)
             return carry
 
-        profiles(0, 0)
-        lax.fori_loop(1, pairs, render, 0)
-        add_image(0, pairs - 1)
-        profiles(1, pairs - 1)
-        add_image(1, pairs - 1)
+        lax.fori_loop(0, chunks // together, add_image, 0)
 
         for j in range(ng):
             isend[s, j] = image[j * rows : (j + 1) * rows, :].astype(isend.dtype)
@@ -320,51 +320,78 @@
         whole_t[0] = whole[s].reshape(PIX, PIX)
         whole_t[1] = whole_t[0].T
 
-        def backward(j, carry):
-            for half in range(2):
-                sides = ((0, pus, whole_t[0], pvs), (1, pvs, whole_t[1], pus))
-                for uv, own, matrix, other in sides:
-                    weighted = jnp.dot(matrix, other[half][j], preferred_element_type=jnp.float32)
-                    for t in range(BLK // 128):
-                        g = (2 * j + half) * (BLK // 128) + t
-                        b, row = g // TILES, g % TILES
-                        lanes = slice(t * 128, (t + 1) * 128)
-                        d = pixels[...] - proj[b, uv, pl.ds(row, 1), :]
-                        total = own[half][j, :, lanes].astype(jnp.float32) * d * weighted[:, lanes]
-                        gown[pl.ds(uv * tiles + g, 1), :] = curve[1, pl.ds(g, 1), :] * jnp.sum(
-                            total, axis=0, keepdims=True
+        def backward(c, carry):
+            def part(k, carry):
+                for half in range(2):
+                    at = (2 * k + half) * BLK
+                    cols = pl.ds(pl.multiple_of(at, BLK), BLK)
+                    for uv, own, matrix, other in ((0, pu, whole_t[0], pv), (1, pv, whole_t[1], pu)):
+                        weighted = jnp.dot(
+                            matrix, other[c, :, cols], preferred_element_type=jnp.float32
                         )
+                        for t in range(BLK // 128):
+                            tile = (2 * k + half) * (BLK // 128) + t
+                            g = c * CTILES + tile
+                            col = pl.ds(pl.multiple_of(at + t * 128, 128), 128)
+                            d = pixels[...] - proj[g // TILES, uv, pl.ds(g % TILES, 1), :]
+                            total = (
+                                own[c, :, col].astype(jnp.float32)
+                                * d
+                                * weighted[:, t * 128 : (t + 1) * 128]
+                            )
+                            gown[pl.ds(uv * CTILES + tile, 1), :] = curve[
+                                1, pl.ds(g, 1), :
+                            ] * jnp.sum(total, axis=0, keepdims=True)
+                return carry
+
+            lax.fori_loop(0, CHUNK // (2 * BLK), part, 0)
+            gsend[s, c] = gown[...].astype(jnp.bfloat16)
+            send_all(
+                "img",
+                lambda peer: gsend.at[s, c],
+                lambda me, r: grecv.at[s, c, me],
+                g_sem.at[s, c],
+            )
+            grecv[s, c, ib] = gsend[s, c]
             return carry
 
-        lax.fori_loop(0, pairs, backward, 0)
-
-        gsend[s] = gown[...].astype(jnp.bfloat16)
-        send_all("img", lambda peer: gsend.at[s], lambda me, r: grecv.at[s, me], g_sem.at[s])
-        grecv[s, ib] = gsend[s]
-        wait_for(grecv.at[s, pl.ds(0, ni - 1)], g_sem.at[s, 1])
-        gall[...] = grecv[s].astype(jnp.float32)
-
-        def gradient(i):
-            return gall[i % ni, (i // ni) * tiles : (i // ni + 1) * tiles, :]
-
-        squares = jnp.zeros((8, 128), jnp.float32)
-        for i in range(2 * ni):
-            gi = gradient(i)
-            for k in range(i, 2 * ni):
-                product = (gi * gradient(k)).reshape(tiles // 8, 8, 128)
-                squares = squares + weights[i, k] * jnp.sum(product, axis=0)
-        s2[s, gj] = squares
+        lax.fori_loop(0, chunks, backward, 0)
+
+        def gradient(c, i):
+            return gall[c, i % ni, (i // ni) * CTILES : (i // ni + 1) * CTILES, :]
+
+        def add_squares(c, squares):
+            wait_for(grecv.at[s, c, pl.ds(0, ni - 1)], g_sem.at[s, c, 1])
+            gall[c] = grecv[s, c].astype(jnp.float32)
+            for i in range(2 * ni):
+                gi = gradient(c, i)
+                for k in range(i, 2 * ni):
+                    product = gi * gradient(c, k)
+                    squares = squares + weights[i, k] * jnp.sum(
+                        product.reshape(CTILES // 8, 8, 128), axis=0
+                    )
+            return squares
+
+        squares = lax.fori_loop(0, chunks, add_squares, jnp.zeros((8, 128), jnp.float32))
+        s2[s, gj] = jnp.sum(squares, axis=0, keepdims=True)
         send_all("gauss", lambda peer: s2.at[s, gj], lambda me, r: s2.at[s, me], s2_sem.at[s])
         if s == 0:
-            for uv in range(2):
-                moved = jnp.zeros((ni, TILES, 128), jnp.float32)
-                for i in range(2 * ni):
-                    moved = moved + weights[2 * ni + uv, i] * gradient(i).reshape(ni, TILES, 128)
-                shift[:, uv] = moved
+
+            def move(c, carry):
+                for uv in range(2):
+                    moved = jnp.zeros((SUBS, TILES, 128), jnp.float32)
+                    for i in range(2 * ni):
+                        moved = moved + weights[2 * ni + uv, i] * gradient(c, i).reshape(
+                            SUBS, TILES, 128
+                        )
+                    shift[pl.ds(c * SUBS, SUBS), uv] = moved
+                return carry
+
+            lax.fori_loop(0, chunks, move, 0)
         for b in range(ni):
             for uv in range(2):
-                first = pl.multiple_of(uv * tiles + ib * TILES, TILES)
-                gpart[b, uv] = gall[b, pl.ds(first, TILES), :]
+                first = pl.multiple_of(uv * CTILES + (ib % SUBS) * TILES, TILES)
+                gpart[b, uv] = gall[ib // SUBS, b, pl.ds(first, TILES), :]
         for uv in range(2):
             for t in range(TILES):
                 grads[uv * ni : (uv + 1) * ni, t * 128 : (t + 1) * 128] = gpart[:, uv, t, :]
@@ -391,7 +418,8 @@
         wait_for(arecv.at[s, pl.ds(0, ni - 1)], a_sem.at[s, 0])
         wait_for(irecv.at[s], i_sem.at[s, 0])
         wait_for(whole.at[s, pl.ds(0, ng - 1)], r_sem.at[s, 0])
-        wait_for(grecv.at[s, pl.ds(0, ni - 1)], g_sem.at[s, 0])
+        for c in range(chunks):
+            wait_for(grecv.at[s, c, pl.ds(0, ni - 1)], g_sem.at[s, c, 0])
         wait_for(s2.at[s, pl.ds(0, ng - 1)], s2_sem.at[s, 0])
     pltpu.make_async_copy(resid, res_hbm, out_sem.at[0]).wait()
     done.wait()
@@ -403,7 +431,7 @@
     ng, ni = lax.axis_size("gauss"), lax.axis_size("img")
     rows = PIX // ng
     count = ni * SUB
-    pairs = count // BLK // 2
+    chunks = count // CHUNK
     f32, b16 = jnp.float32, jnp.bfloat16
     vmem, hbm, smem = (
         pl.BlockSpec(memory_space=m) for m in (pltpu.VMEM, pl.ANY, pltpu.SMEM)
@@ -435,10 +463,8 @@
             pltpu.VMEM((2 * ni + 8, 2 * ni), f32),
             pltpu.VMEM((ni, 2, TILES, 128), f32),
             pltpu.VMEM((PIX, 128), f32),
-            pltpu.VMEM((pairs, PIX, BLK), b16),
-            pltpu.VMEM((pairs, PIX, BLK), b16),
-            pltpu.VMEM((pairs, PIX, BLK), b16),
-            pltpu.VMEM((pairs, PIX, BLK), b16),
+            pltpu.VMEM((chunks, PIX, CHUNK), b16),
+            pltpu.VMEM((chunks, PIX, CHUNK), b16),
             pltpu.VMEM((PIX, PIX), f32),
             pltpu.VMEM((STEPS, ng, rows, PIX), b16),
             pltpu.VMEM((STEPS, ng - 1, rows, PIX), b16),
@@ -447,13 +473,13 @@
             pltpu.VMEM((STEPS, ng, rows, PIX), b16),
             pltpu.VMEM((2, PIX, PIX), b16),
             pltpu.VMEM((2 * ni, SUB), f32),
-            pltpu.VMEM((2 * count // 128, 128), f32),
-            pltpu.VMEM((STEPS, 2 * count // 128, 128), b16),
-            pltpu.VMEM((STEPS, ni, 2 * count // 128, 128), b16),
-            pltpu.VMEM((ni, 2 * count // 128, 128), f32),
+            pltpu.VMEM((2 * CTILES, 128), f32),
+            pltpu.VMEM((STEPS, chunks, 2 * CTILES, 128), b16),
+            pltpu.VMEM((STEPS, chunks, ni, 2 * CTILES, 128), b16),
+            pltpu.VMEM((chunks, ni, 2 * CTILES, 128), f32),
             pltpu.VMEM((ni, 2, TILES, 128), f32),
             pltpu.VMEM((STEPS, 3 * K, SUB), f32),
-            pltpu.VMEM((STEPS, ng, 8, 128), f32),
+            pltpu.VMEM((STEPS, ng, 1, 128), f32),
             pltpu.VMEM((3 * K, SUB), f32),
             dma((5,)),
             dma((2,)),
@@ -461,7 +487,7 @@
             dma((STEPS, 2)),
             dma((STEPS, 2)),
             dma((STEPS, 2)),
-            dma((STEPS, 2)),
+            dma((STEPS, chunks, 2)),
             dma((STEPS, 2)),
         ],
         compiler_params=pltpu.CompilerParams(

time: 83.8 us -> 79.4 us (0.947)
  Pallas kernels: 80 us -> 75.6 us
    pallas_call x1, Pallas kernels: 80 us -> 75.6 us  [body(): pl.pallas_call(functools.partial(kernel, ng, ni), out_shape=(jax.ShapeDty...]
where the time goes in v3:
time: 79.4 us; the launch traced here: 79.1 us
  Pallas kernels  75.6 us (95%)
  local copies, waits for them, and re-layouts  2.94 us (4%)
    pallas_call x1, Pallas kernels, body(): pl.pallas_call(functools.partial(kernel, ng, ni), out_shape=(jax.ShapeDty...  75.6 us
    unnamed x2, local copies, waits for them, and re-layouts  2.94 us

profile of v3, /device:TPU:1, one launch (start us, length us, event | category | flops | bytes accessed | tf_op | source)
XLA Modules:
  0.0 79.1 jit_solution(6436123751453086229)
XLA Ops:
  0.6 75.6 %shard_map.95 = (f32[16,256]{1,0:T(8,128)}, f32[48,1024]{1,0:T(8,128)}) custom-call(s32[4]{0:T(128)} %pose_ref.1, s32[4]{0:T(128)} %order_ref.1, f32[4,16]{1,0:T(4,128)} %lat_ref.1, bf16[4,16,256]{2,1,0:T(8,128)(2,1)} %obs_hbm.1, f32[3,8192]{1,0:T(4,128)} %base_hbm.1, f32[64,128]{1,0:T(8,128)} %bitcast.11, f32[64,128]{1,0:T(8,128)} %bitcast.12, ...), custom_call_target="tpu_custom_call" | custom-call | tf_op jit(solution)/shard_map/pallas_call | solution.py:440
  76.2 1.3 %copy.12 = f32[1,16,256]{2,1,0:T(8,128)} copy(f32[1,16,256]{2,1,0:T(8,128)} %bitcast.13) | data formatting | bytes 32768
  77.5 1.6 %copy.13 = f32[16,3,1024]{2,0,1:T(8,128)} copy(f32[16,3,1024]{2,0,1:T(8,128)} %bitcast.9) | data formatting | bytes 393216

commit v4 on v3

--- a/solution.py
+++ b/solution.py
@@ -17,7 +17,7 @@
 CHUNK = 2048
 SUBS = CHUNK // SUB
 CTILES = CHUNK // 128
-BLK = 512
+BLK = 1024
 CENTER = (PIX - 1) * 0.5
 
 step_size = 0.5
@@ -76,16 +76,19 @@
 def kernel(
     ng,
     ni,
-    pose_ref,
-    order_ref,
-    lat_ref,
+    pose_hbm,
+    order_hbm,
+    lat_hbm,
     obs_hbm,
     base_hbm,
     amp_hbm,
     wid_hbm,
     modes_hbm,
-    res_hbm,
-    new_hbm,
+    final,
+    newv,
+    pose_ref,
+    order_ref,
+    lat_ref,
     zpad,
     obs,
     rows_in,
@@ -105,10 +108,11 @@
     pixels,
     pu,
     pv,
+    slope_u,
+    slope_v,
     image,
     isend,
     irecv,
-    resid,
     rsend,
     whole,
     whole_t,
@@ -120,9 +124,7 @@
     gpart,
     mgrad,
     s2,
-    newv,
     in_sem,
-    out_sem,
     p_sem,
     a_sem,
     i_sem,
@@ -136,7 +138,21 @@
     gj = lax.axis_index("gauss")
     ib = lax.axis_index("img")
 
+    def partner(axis, n, r):
+        me = ib if axis == "img" else gj
+        return lax.rem(me + (n // 2 + r if r < n // 2 else n - r), n)
+
+    barrier = pltpu.get_barrier_semaphore()
+    for axis, n in (("gauss", ng), ("img", ni)):
+        for r in range(1, n):
+            pl.semaphore_signal(
+                barrier, inc=1, device_id={axis: partner(axis, n, r)}, device_id_type=MESH
+            )
+
     loads = [
+        pltpu.make_async_copy(pose_hbm, pose_ref, in_sem.at[5]),
+        pltpu.make_async_copy(order_hbm, order_ref, in_sem.at[6]),
+        pltpu.make_async_copy(lat_hbm, lat_ref, in_sem.at[7]),
         pltpu.make_async_copy(modes_hbm, rows_in.at[pl.ds(0, 3 * K)], in_sem.at[0]),
         pltpu.make_async_copy(
             base_hbm.at[:, pl.ds(pl.multiple_of(ib * SUB, SUB), SUB)], base_in, in_sem.at[1]
@@ -148,17 +164,9 @@
     for copy in loads:
         copy.start()
 
-    def partner(axis, n, r):
-        me = ib if axis == "img" else gj
-        return lax.rem(me + (n // 2 + r if r < n // 2 else n - r), n)
-
-    barrier = pltpu.get_barrier_semaphore()
-    for axis, n in (("gauss", ng), ("img", ni)):
-        for r in range(1, n):
-            pl.semaphore_signal(
-                barrier, inc=1, device_id={axis: partner(axis, n, r)}, device_id_type=MESH
-            )
-
+    for copy in loads[:3]:
+        copy.wait()
+    del loads[:3]
     zpad[...] = jnp.zeros_like(zpad)
     zpad[0:4, 0:K] = lat_ref[...]
     chosen = [order_ref[s] for s in range(STEPS)]
@@ -258,7 +266,7 @@
         lax.fori_loop(1 if s == 0 else 0, ni, render, 0)
 
         image[...] = jnp.zeros_like(image)
-        together = 2 if chunks % 2 == 0 else 1
+        together = 4 if chunks % 4 == 0 else 1
 
         def add_image(i, carry):
             terms = [
@@ -287,6 +295,17 @@
             loads[4].wait()
         measured = obs[chosen[s]].astype(jnp.float32)
         total = image[pl.ds(pl.multiple_of(gj * rows, rows), rows), :] - measured
+        def slopes(b, carry):
+            for t in range(TILES):
+                first = pl.multiple_of((b % SUBS) * SUB + t * 128, 128)
+                for uv, own, slope in ((0, pu, slope_u), (1, pv, slope_v)):
+                    d = pixels[...] - proj[b, uv, t : t + 1, :]
+                    slope[b // SUBS, :, pl.ds(first, 128)] = (
+                        own[b // SUBS, :, pl.ds(first, 128)].astype(jnp.float32) * d
+                    )
+            return carry
+
+        lax.fori_loop(0, ni, slopes, 0)
         cross = coefficients(s)[:, : 3 * K]
         other = jnp.concatenate([cross, psend[:, : 3 * K]], axis=0)
         wmat[...] = lax.dot_general(
@@ -314,8 +333,7 @@
         send_all("gauss", lambda peer: rsend.at[s], lambda me, r: whole.at[s, me], r_sem.at[s])
         whole[s, gj] = rsend[s]
         if s == STEPS - 1:
-            resid[...] = total
-            pltpu.make_async_copy(resid, res_hbm, out_sem.at[0]).start()
+            final[...] = total
         wait_for(whole.at[s, pl.ds(0, ng - 1)], r_sem.at[s, 1])
         whole_t[0] = whole[s].reshape(PIX, PIX)
         whole_t[1] = whole_t[0].T
@@ -325,7 +343,10 @@
                 for half in range(2):
                     at = (2 * k + half) * BLK
                     cols = pl.ds(pl.multiple_of(at, BLK), BLK)
-                    for uv, own, matrix, other in ((0, pu, whole_t[0], pv), (1, pv, whole_t[1], pu)):
+                    for uv, slope, matrix, other in (
+                        (0, slope_u, whole_t[0], pv),
+                        (1, slope_v, whole_t[1], pu),
+                    ):
                         weighted = jnp.dot(
                             matrix, other[c, :, cols], preferred_element_type=jnp.float32
                         )
@@ -333,12 +354,7 @@
                             tile = (2 * k + half) * (BLK // 128) + t
                             g = c * CTILES + tile
                             col = pl.ds(pl.multiple_of(at + t * 128, 128), 128)
-                            d = pixels[...] - proj[g // TILES, uv, pl.ds(g % TILES, 1), :]
-                            total = (
-                                own[c, :, col].astype(jnp.float32)
-                                * d
-                                * weighted[:, t * 128 : (t + 1) * 128]
-                            )
+                            total = slope[c, :, col] * weighted[:, t * 128 : (t + 1) * 128]
                             gown[pl.ds(uv * CTILES + tile, 1), :] = curve[
                                 1, pl.ds(g, 1), :
                             ] * jnp.sum(total, axis=0, keepdims=True)
@@ -410,8 +426,6 @@
         halves.append(step_size / jnp.sqrt(sums * (1.0 / entries) + tiny_eps))
 
     newv[...] = newv[...] - halves[1] * mgrad[1]
-    done = pltpu.make_async_copy(newv, new_hbm, out_sem.at[1])
-    done.start()
 
     wait_for(params.at[pl.ds(0, ni - 1)], p_sem.at[0])
     for s in range(STEPS):
@@ -421,8 +435,6 @@
         for c in range(chunks):
             wait_for(grecv.at[s, c, pl.ds(0, ni - 1)], g_sem.at[s, c, 0])
         wait_for(s2.at[s, pl.ds(0, ng - 1)], s2_sem.at[s, 0])
-    pltpu.make_async_copy(resid, res_hbm, out_sem.at[0]).wait()
-    done.wait()
 
 
 def body(
@@ -433,9 +445,8 @@
     count = ni * SUB
     chunks = count // CHUNK
     f32, b16 = jnp.float32, jnp.bfloat16
-    vmem, hbm, smem = (
-        pl.BlockSpec(memory_space=m) for m in (pltpu.VMEM, pl.ANY, pltpu.SMEM)
-    )
+    hbm, vmem = (pl.BlockSpec(memory_space=m) for m in (pltpu.HBM, pltpu.VMEM))
+    held = functools.partial(pltpu.with_memory_space_constraint, memory_space=pltpu.HBM)
     dma = pltpu.SemaphoreType.DMA
     final, new = pl.pallas_call(
         functools.partial(kernel, ng, ni),
@@ -443,9 +454,12 @@
             jax.ShapeDtypeStruct((rows, PIX), f32),
             jax.ShapeDtypeStruct((3 * K, SUB), f32),
         ),
-        in_specs=[smem, smem, vmem, hbm, hbm, hbm, hbm, hbm],
-        out_specs=(hbm, hbm),
+        in_specs=[hbm] * 8,
+        out_specs=(vmem, vmem),
         scratch_shapes=[
+            pltpu.SMEM(pose_index.shape, jnp.int32),
+            pltpu.SMEM(batch_order.shape, jnp.int32),
+            pltpu.VMEM(latents.shape, f32),
             pltpu.VMEM((8, 128), f32),
             pltpu.VMEM((4, rows, PIX), b16),
             pltpu.VMEM((3 * K + 8, SUB), f32),
@@ -465,10 +479,11 @@
             pltpu.VMEM((PIX, 128), f32),
             pltpu.VMEM((chunks, PIX, CHUNK), b16),
             pltpu.VMEM((chunks, PIX, CHUNK), b16),
+            pltpu.VMEM((chunks, PIX, CHUNK), f32),
+            pltpu.VMEM((chunks, PIX, CHUNK), f32),
             pltpu.VMEM((PIX, PIX), f32),
             pltpu.VMEM((STEPS, ng, rows, PIX), b16),
             pltpu.VMEM((STEPS, ng - 1, rows, PIX), b16),
-            pltpu.VMEM((rows, PIX), f32),
             pltpu.VMEM((STEPS, rows, PIX), b16),
             pltpu.VMEM((STEPS, ng, rows, PIX), b16),
             pltpu.VMEM((2, PIX, PIX), b16),
@@ -480,9 +495,7 @@
             pltpu.VMEM((ni, 2, TILES, 128), f32),
             pltpu.VMEM((STEPS, 3 * K, SUB), f32),
             pltpu.VMEM((STEPS, ng, 1, 128), f32),
-            pltpu.VMEM((3 * K, SUB), f32),
-            dma((5,)),
-            dma((2,)),
+            dma((8,)),
             dma((2,)),
             dma((STEPS, 2)),
             dma((STEPS, 2)),
@@ -491,17 +504,17 @@
             dma((STEPS, 2)),
         ],
         compiler_params=pltpu.CompilerParams(
-            collective_id=0, has_side_effects=True, vmem_limit_bytes=60 * 2**20
+            collective_id=0, has_side_effects=True, vmem_limit_bytes=40 * 2**20
         ),
     )(
-        pose_index,
-        batch_order,
-        latents,
-        observed,
-        base_positions,
-        amplitudes.reshape(count // 128, 128),
-        widths.reshape(count // 128, 128),
-        deform_modes.transpose(1, 0, 2).reshape(3 * K, SUB),
+        held(pose_index),
+        held(batch_order),
+        held(latents),
+        held(observed),
+        held(base_positions),
+        held(amplitudes.reshape(count // 128, 128)),
+        held(widths.reshape(count // 128, 128)),
+        held(deform_modes.transpose(1, 0, 2).reshape(3 * K, SUB)),
     )
     return final[None], new.reshape(3, K, SUB).transpose(1, 0, 2)
 

time: 79.4 us -> 72.7 us (0.916)
  Pallas kernels: 75.6 us -> 70.6 us
  local copies, waits for them, and re-layouts: 2.94 us -> 1.28 us
    pallas_call x1, Pallas kernels: 75.6 us -> 70.6 us  [body(): pl.pallas_call(functools.partial(kernel, ng, ni), out_shape=(jax.ShapeDty...]
    unnamed x2, local copies, waits for them, and re-layouts: 2.94 us -> 1.28 us
where the time goes in v4:
time: 72.7 us; the launch traced here: 72.6 us
  Pallas kernels  70.6 us (97%)
  local copies, waits for them, and re-layouts  1.28 us (2%)
    pallas_call x1, Pallas kernels, body(): pl.pallas_call(functools.partial(kernel, ng, ni), out_shape=(jax.ShapeDty...  70.6 us

profile of v4, /device:TPU:1, one launch (start us, length us, event | category | flops | bytes accessed | tf_op | source)
XLA Modules:
  0.0 72.6 jit_solution(2855355982633738851)
XLA Ops:
  0.6 70.6 %shard_map.95 = (f32[16,256]{1,0:T(8,128)S(1)}, f32[48,1024]{1,0:T(8,128)S(1)}) custom-call(s32[4]{0:T(128)} %pose_hbm.1, s32[4]{0:T(128)} %order_hbm.1, f32[4,16]{1,0:T(4,128)} %lat_hbm.1, bf16[4,16,256]{2,1,0:T(8,128)(2,1)} %obs_hbm.1, f32[3,8192]{1,0:T(4,128)} %base_hbm.1, f32[64,128]{1,0:T(8,128)} %bitcast.12, f32[64,128]{1,0:T(8,128)} %bitcast.13, ...), custom_call_target="tpu_custom_call" | custom-call | tf_op jit(solution)/shard_map/pallas_call | solution.py:451
  71.3 0.6 copy.12
  71.9 0.7 copy.13

commit v5 on v4

--- a/solution.py
+++ b/solution.py
@@ -84,8 +84,7 @@
     amp_hbm,
     wid_hbm,
     modes_hbm,
-    final,
-    newv,
+    both,
     pose_ref,
     order_ref,
     lat_ref,
@@ -172,9 +171,9 @@
     chosen = [order_ref[s] for s in range(STEPS)]
     psend[...] = jnp.zeros_like(psend)
     for s in range(STEPS):
-        both = own_coefficients(pose_ref[chosen[s]], zpad[pl.ds(chosen[s], 1), :])
-        psend[2 * s : 2 * s + 1, :] = both[0]
-        psend[2 * s + 1 : 2 * s + 2, :] = both[1]
+        pair = own_coefficients(pose_ref[chosen[s]], zpad[pl.ds(chosen[s], 1), :])
+        psend[2 * s : 2 * s + 1, :] = pair[0]
+        psend[2 * s + 1 : 2 * s + 2, :] = pair[1]
     params[ib] = psend[...]
 
     pl.semaphore_wait(barrier, ni + ng - 2)
@@ -238,17 +237,21 @@
     halves = []
 
     for s in range(STEPS):
+        def side_by_side(ref, first, n):
+            return jnp.concatenate([ref[first + t] for t in range(n)], axis=1)
+
         def profiles(b):
             for t in range(TILES):
                 g = b * TILES + t
                 c = curve[0, pl.ds(g, 1), :]
-                first = pl.multiple_of((b % SUBS) * SUB + t * 128, 128)
-                d = pixels[...] - proj[b, 0, t : t + 1, :]
-                pu[b // SUBS, :, pl.ds(first, 128)] = jnp.exp2(d * d * c).astype(jnp.bfloat16)
-                d = pixels[...] - proj[b, 1, t : t + 1, :]
-                pv[b // SUBS, :, pl.ds(first, 128)] = (
-                    amp[pl.ds(g, 1), :] * jnp.exp2(d * d * c)
-                ).astype(jnp.bfloat16)
+                u, v = proj[b, 0, t : t + 1, :], proj[b, 1, t : t + 1, :]
+                a = amp[pl.ds(g, 1), :]
+                for m in range(0, PIX, 16):
+                    part = slice(m, m + 16)
+                    d = pixels[part] - u
+                    pu[g, part] = jnp.exp2(d * d * c).astype(jnp.bfloat16)
+                    d = pixels[part] - v
+                    pv[g, part] = (a * jnp.exp2(d * d * c)).astype(jnp.bfloat16)
 
         if s == 0:
             proj[ib] = arecv[0, ib]
@@ -271,8 +274,8 @@
         def add_image(i, carry):
             terms = [
                 lax.dot_general(
-                    pu[i * together + k],
-                    pv[i * together + k],
+                    side_by_side(pu, (i * together + k) * CTILES, CTILES),
+                    side_by_side(pv, (i * together + k) * CTILES, CTILES),
                     (((1,), (1,)), ((), ())),
                     preferred_element_type=jnp.float32,
                 )
@@ -297,12 +300,10 @@
         total = image[pl.ds(pl.multiple_of(gj * rows, rows), rows), :] - measured
         def slopes(b, carry):
             for t in range(TILES):
-                first = pl.multiple_of((b % SUBS) * SUB + t * 128, 128)
+                g = b * TILES + t
                 for uv, own, slope in ((0, pu, slope_u), (1, pv, slope_v)):
                     d = pixels[...] - proj[b, uv, t : t + 1, :]
-                    slope[b // SUBS, :, pl.ds(first, 128)] = (
-                        own[b // SUBS, :, pl.ds(first, 128)].astype(jnp.float32) * d
-                    )
+                    slope[g] = own[g].astype(jnp.float32) * d
             return carry
 
         lax.fori_loop(0, ni, slopes, 0)
@@ -333,7 +334,7 @@
         send_all("gauss", lambda peer: rsend.at[s], lambda me, r: whole.at[s, me], r_sem.at[s])
         whole[s, gj] = rsend[s]
         if s == STEPS - 1:
-            final[...] = total
+            both[3 * K :, :PIX] = total
         wait_for(whole.at[s, pl.ds(0, ng - 1)], r_sem.at[s, 1])
         whole_t[0] = whole[s].reshape(PIX, PIX)
         whole_t[1] = whole_t[0].T
@@ -341,20 +342,20 @@
         def backward(c, carry):
             def part(k, carry):
                 for half in range(2):
-                    at = (2 * k + half) * BLK
-                    cols = pl.ds(pl.multiple_of(at, BLK), BLK)
+                    at = (2 * k + half) * (BLK // 128)
                     for uv, slope, matrix, other in (
                         (0, slope_u, whole_t[0], pv),
                         (1, slope_v, whole_t[1], pu),
                     ):
                         weighted = jnp.dot(
-                            matrix, other[c, :, cols], preferred_element_type=jnp.float32
+                            matrix,
+                            side_by_side(other, c * CTILES + at, BLK // 128),
+                            preferred_element_type=jnp.float32
                         )
                         for t in range(BLK // 128):
-                            tile = (2 * k + half) * (BLK // 128) + t
+                            tile = at + t
                             g = c * CTILES + tile
-                            col = pl.ds(pl.multiple_of(at + t * 128, 128), 128)
-                            total = slope[c, :, col] * weighted[:, t * 128 : (t + 1) * 128]
+                            total = slope[g] * weighted[:, t * 128 : (t + 1) * 128]
                             gown[pl.ds(uv * CTILES + tile, 1), :] = curve[
                                 1, pl.ds(g, 1), :
                             ] * jnp.sum(total, axis=0, keepdims=True)
@@ -419,13 +420,13 @@
             preferred_element_type=jnp.float32,
         )
         if s == 1:
-            newv[...] = rows_in[: 3 * K, :] - halves[0] * mgrad[0]
+            both[: 3 * K, :] = rows_in[: 3 * K, :] - halves[0] * mgrad[0]
         wait_for(s2.at[s, pl.ds(0, ng - 1)], s2_sem.at[s, 1])
         sums = jnp.sum(s2[s], axis=0)
         sums = jnp.sum(jnp.sum(sums, axis=0, keepdims=True), axis=1, keepdims=True)
         halves.append(step_size / jnp.sqrt(sums * (1.0 / entries) + tiny_eps))
 
-    newv[...] = newv[...] - halves[1] * mgrad[1]
+    both[: 3 * K, :] = both[: 3 * K, :] - halves[1] * mgrad[1]
 
     wait_for(params.at[pl.ds(0, ni - 1)], p_sem.at[0])
     for s in range(STEPS):
@@ -448,14 +449,11 @@
     hbm, vmem = (pl.BlockSpec(memory_space=m) for m in (pltpu.HBM, pltpu.VMEM))
     held = functools.partial(pltpu.with_memory_space_constraint, memory_space=pltpu.HBM)
     dma = pltpu.SemaphoreType.DMA
-    final, new = pl.pallas_call(
+    both = pl.pallas_call(
         functools.partial(kernel, ng, ni),
-        out_shape=(
-            jax.ShapeDtypeStruct((rows, PIX), f32),
-            jax.ShapeDtypeStruct((3 * K, SUB), f32),
-        ),
+        out_shape=jax.ShapeDtypeStruct((3 * K + rows, SUB), f32),
         in_specs=[hbm] * 8,
-        out_specs=(vmem, vmem),
+        out_specs=vmem,
         scratch_shapes=[
             pltpu.SMEM(pose_index.shape, jnp.int32),
             pltpu.SMEM(batch_order.shape, jnp.int32),
@@ -477,10 +475,10 @@
             pltpu.VMEM((2 * ni + 8, 2 * ni), f32),
             pltpu.VMEM((ni, 2, TILES, 128), f32),
             pltpu.VMEM((PIX, 128), f32),
-            pltpu.VMEM((chunks, PIX, CHUNK), b16),
-            pltpu.VMEM((chunks, PIX, CHUNK), b16),
-            pltpu.VMEM((chunks, PIX, CHUNK), f32),
-            pltpu.VMEM((chunks, PIX, CHUNK), f32),
+            pltpu.VMEM((count // 128, PIX, 128), b16),
+            pltpu.VMEM((count // 128, PIX, 128), b16),
+            pltpu.VMEM((count // 128, PIX, 128), f32),
+            pltpu.VMEM((count // 128, PIX, 128), f32),
             pltpu.VMEM((PIX, PIX), f32),
             pltpu.VMEM((STEPS, ng, rows, PIX), b16),
             pltpu.VMEM((STEPS, ng - 1, rows, PIX), b16),
@@ -516,7 +514,8 @@
         held(widths.reshape(count // 128, 128)),
         held(deform_modes.transpose(1, 0, 2).reshape(3 * K, SUB)),
     )
-    return final[None], new.reshape(3, K, SUB).transpose(1, 0, 2)
+    new = both[: 3 * K].reshape(3, K, SUB).transpose(1, 0, 2)
+    return both[None, 3 * K :, :PIX], new
 
 
 def solution(mesh):

time: 72.7 us -> 72.3 us (level)
    unnamed x2 -> x0, local copies, waits for them, and re-layouts: 1.28 us -> none
where the time goes in v5:
time: 72.3 us; the launch traced here: 72.2 us
  Pallas kernels  70.2 us (97%)
  local copies, waits for them, and re-layouts  1.3 us (2%)
    pallas_call x1, Pallas kernels, body(): pl.pallas_call(functools.partial(kernel, ng, ni), out_shape=jax.ShapeDtyp...  70.2 us

profile of v5, /device:TPU:1, one launch (start us, length us, event | category | flops | bytes accessed | tf_op | source)
XLA Modules:
  0.0 72.2 jit_solution(15749069141773415254)
XLA Ops:
  0.6 70.2 %shard_map.95 = f32[64,1024]{1,0:T(8,128)S(1)} custom-call(s32[4]{0:T(128)} %pose_hbm.1, s32[4]{0:T(128)} %order_hbm.1, f32[4,16]{1,0:T(4,128)} %lat_hbm.1, bf16[4,16,256]{2,1,0:T(8,128)(2,1)} %obs_hbm.1, f32[3,8192]{1,0:T(4,128)} %base_hbm.1, f32[64,128]{1,0:T(8,128)} %bitcast.12, f32[64,128]{1,0:T(8,128)} %bitcast.13, f32[48,1024]{1,0:T(8,128)} %bitcast.11), custom_call_target="tpu_custom_call" | custom-call | tf_op jit(solution)/shard_map/pallas_call | solution.py:452
  70.9 0.6 slice_bitcast_fusion
  71.5 0.7 slice.7

commit v6 on v5

--- a/solution.py
+++ b/solution.py
@@ -336,16 +336,15 @@
         if s == STEPS - 1:
             both[3 * K :, :PIX] = total
         wait_for(whole.at[s, pl.ds(0, ng - 1)], r_sem.at[s, 1])
-        whole_t[0] = whole[s].reshape(PIX, PIX)
-        whole_t[1] = whole_t[0].T
+        whole_t[...] = whole[s].reshape(PIX, PIX).T
 
         def backward(c, carry):
             def part(k, carry):
                 for half in range(2):
                     at = (2 * k + half) * (BLK // 128)
                     for uv, slope, matrix, other in (
-                        (0, slope_u, whole_t[0], pv),
-                        (1, slope_v, whole_t[1], pu),
+                        (0, slope_u, whole[s].reshape(PIX, PIX), pv),
+                        (1, slope_v, whole_t[...], pu),
                     ):
                         weighted = jnp.dot(
                             matrix,
@@ -484,7 +483,7 @@
             pltpu.VMEM((STEPS, ng - 1, rows, PIX), b16),
             pltpu.VMEM((STEPS, rows, PIX), b16),
             pltpu.VMEM((STEPS, ng, rows, PIX), b16),
-            pltpu.VMEM((2, PIX, PIX), b16),
+            pltpu.VMEM((PIX, PIX), b16),
             pltpu.VMEM((2 * ni, SUB), f32),
             pltpu.VMEM((2 * CTILES, 128), f32),
             pltpu.VMEM((STEPS, chunks, 2 * CTILES, 128), b16),

time: 72.3 us -> 72.3 us (level)
  no operation moved by 1% of the time
where the time goes in v6:
time: 72.3 us; the launch traced here: 72.2 us
  Pallas kernels  70.2 us (97%)
  local copies, waits for them, and re-layouts  1.3 us (2%)
    pallas_call x1, Pallas kernels, body(): pl.pallas_call(functools.partial(kernel, ng, ni), out_shape=jax.ShapeDtyp...  70.2 us

profile of v6, /device:TPU:1, one launch (start us, length us, event | category | flops | bytes accessed | tf_op | source)
XLA Modules:
  0.0 72.2 jit_solution(5881442075068780182)
XLA Ops:
  0.6 70.2 %shard_map.95 = f32[64,1024]{1,0:T(8,128)S(1)} custom-call(s32[4]{0:T(128)} %pose_hbm.1, s32[4]{0:T(128)} %order_hbm.1, f32[4,16]{1,0:T(4,128)} %lat_hbm.1, bf16[4,16,256]{2,1,0:T(8,128)(2,1)} %obs_hbm.1, f32[3,8192]{1,0:T(4,128)} %base_hbm.1, f32[64,128]{1,0:T(8,128)} %bitcast.12, f32[64,128]{1,0:T(8,128)} %bitcast.13, f32[48,1024]{1,0:T(8,128)} %bitcast.11), custom_call_target="tpu_custom_call" | custom-call | tf_op jit(solution)/shard_map/pallas_call | solution.py:451
  70.9 0.6 slice_bitcast_fusion
  71.5 0.7 slice.7
